TPU v7x, 32 devices: a whole 2x2x4 slice. The times are simulated.
32 devices in a mesh: clip: 8 (over z, x), tm: 4 (over y, core).
Axes of the slice: x: 2, y: 2, z: 4, core: 2. Of those that a mesh axis runs over, the one named last changes fastest.
Arguments:
- mel_frames: bfloat16 [16, 2048, 80], P('clip', 'tm'), may hold values from -6 to 6
- lengths: int32 [16], P('clip'), may hold values from 512 to 2048, as said below
- conv1_weight: bfloat16 [3, 80, 768], P(None, None, 'tm'), may hold values from -0.375 to 0.375
- conv1_bias: bfloat16 [768], P('tm'), may hold values from -1.75 to 1.75
- conv2_weight: bfloat16 [3, 768, 768], P(None, None, 'tm'), may hold values from -0.125 to 0.125
- conv2_bias: bfloat16 [768], P('tm'), may hold values from -1.75 to 1.75
- ln1_gain: bfloat16 [768], P('tm'), may hold values from 0.5 to 1.5
- ln1_bias: bfloat16 [768], P('tm'), may hold values from -1.75 to 1.75
- qkv_weight: bfloat16 [768, 2304], P(None, 'tm'), may hold values from -0.21875 to 0.21875
- q_bias: bfloat16 [768], P('tm'), may hold values from -1.75 to 1.75
- v_bias: bfloat16 [768], P('tm'), may hold values from -0.125 to 0.125
- out_weight: bfloat16 [768, 768], P(None, 'tm'), may hold values from -3.5 to 3.5
- out_bias: bfloat16 [768], P('tm'), may hold values from -1.75 to 1.75
- ln2_gain: bfloat16 [768], P('tm'), may hold values from 0.5 to 1.5
- ln2_bias: bfloat16 [768], P('tm'), may hold values from -1.75 to 1.75
- fc1_weight: bfloat16 [768, 3072], P(None, 'tm'), may hold values from -0.21875 to 0.21875
- fc1_bias: bfloat16 [3072], P('tm'), may hold values from -1.75 to 1.75
- fc2_weight: bfloat16 [3072, 768], P(None, 'tm'), may hold values from -0.109375 to 0.109375
- fc2_bias: bfloat16 [768], P('tm'), may hold values from -1.75 to 1.75
- cotangent: bfloat16 [16, 1024, 768], P('clip', 'tm'), may hold values from -6 to 6
Outputs:
- out_states: bfloat16 [16, 1024, 768], P('clip', 'tm')
- mel_grad: bfloat16 [16, 2048, 80], P('clip', 'tm')
- conv1_weight_grad: float32 [3, 80, 768], P(None, None, 'tm')
- conv1_bias_grad: float32 [768], P('tm')
- conv2_weight_grad: float32 [3, 768, 768], P(None, None, 'tm')
- conv2_bias_grad: float32 [768], P('tm')
- ln1_gain_grad: float32 [768], P('tm')
- ln1_bias_grad: float32 [768], P('tm')
- qkv_weight_grad: float32 [768, 2304], P(None, 'tm')
- q_bias_grad: float32 [768], P('tm')
- v_bias_grad: float32 [768], P('tm')
- out_weight_grad: float32 [768, 768], P(None, 'tm')
- out_bias_grad: float32 [768], P('tm')
- ln2_gain_grad: float32 [768], P('tm')
- ln2_bias_grad: float32 [768], P('tm')
- fc1_weight_grad: float32 [768, 3072], P(None, 'tm')
- fc1_bias_grad: float32 [3072], P('tm')
- fc2_weight_grad: float32 [3072, 768], P(None, 'tm')
- fc2_bias_grad: float32 [768], P('tm')
Inputs may be any that keep to these rules, and one draw needn't show every extreme that they name: `lengths`: in each aligned block of 2 clips (the clips of one index of clip) one clip has all 2048 frames valid; the others vary.
All inputs are finite; a program needn't handle non-finite values.
Results may differ from a plain program's by a relative error of at most 0.018.
Values may be sent and summed in bfloat16 or wider, within the bound.
A program may use at most 192 MiB of HBM per device.

v0:
```python
import math

import jax
import jax.numpy as jnp
from jax import lax
from jax.sharding import PartitionSpec as P

HEADS = 12
HEAD_DIM = 64


def with_halo(array, sides, width):
    for axis, dim in sides:
        size, length = (lax.axis_size(axis), array.shape[dim])
        up = [(i, (i + 1) % size) for i in range(size - 1)]
        down = [(j, i) for i, j in up]
        last = lax.slice_in_dim(array, length - width, length, axis=dim)
        first = lax.slice_in_dim(array, 0, width, axis=dim)
        before = lax.ppermute(last, axis, up)
        after = lax.ppermute(first, axis, down)
        array = jnp.concatenate([before, array, after], axis=dim)
    return array


def passed_along(block, axis, distance):
    devices = range(lax.axis_size(axis))
    route = [(i - distance, i) for i in devices if i - distance in devices]
    return lax.ppermute(block, axis, route)


def gelu_exact(values_in):
    return jax.nn.gelu(values_in, approximate=False)


def gelu_back(values_in, grad_in):
    return jax.vjp(gelu_exact, values_in)[1](grad_in)[0]


def layer_norm(values_in, gain, shift):
    center = values_in - jnp.mean(values_in, axis=-1, keepdims=True)
    spread = jnp.mean(center * center, axis=-1, keepdims=True)
    return center * lax.rsqrt(spread + 1e-05) * gain + shift


def positions(first, count, width):
    half = width // 2
    rates = jnp.exp(-(math.log(10000.0) / (half - 1)) * jnp.arange(half, dtype=jnp.float32))
    angles = (first + jnp.arange(count)).astype(jnp.float32)[:, None] * rates[None, :]
    return jnp.concatenate([jnp.sin(angles), jnp.cos(angles)], axis=1)


def per_device(
    mel_frames,
    lengths,
    conv1_weight,
    conv1_bias,
    conv2_weight,
    conv2_bias,
    ln1_gain,
    ln1_bias,
    qkv_weight,
    q_bias,
    v_bias,
    out_weight,
    out_bias,
    ln2_gain,
    ln2_bias,
    fc1_weight,
    fc1_bias,
    fc2_weight,
    fc2_bias,
    cotangent,
):
    split_axes = (2, 0, 2, 0, 0, 0, 1, 0, 0, 1, 0, 0, 0, 1, 0, 1, 0)
    (
        conv1_weight,
        conv1_bias,
        conv2_weight,
        conv2_bias,
        ln1_gain,
        ln1_bias,
        qkv_weight,
        q_bias,
        v_bias,
        out_weight,
        out_bias,
        ln2_gain,
        ln2_bias,
        fc1_weight,
        fc1_bias,
        fc2_weight,
        fc2_bias,
    ) = (
        lax.all_gather(conv1_weight, "tm", axis=2, tiled=True),
        lax.all_gather(conv1_bias, "tm", axis=0, tiled=True),
        lax.all_gather(conv2_weight, "tm", axis=2, tiled=True),
        lax.all_gather(conv2_bias, "tm", axis=0, tiled=True),
        lax.all_gather(ln1_gain, "tm", axis=0, tiled=True),
        lax.all_gather(ln1_bias, "tm", axis=0, tiled=True),
        lax.all_gather(qkv_weight, "tm", axis=1, tiled=True),
        lax.all_gather(q_bias, "tm", axis=0, tiled=True),
        lax.all_gather(v_bias, "tm", axis=0, tiled=True),
        lax.all_gather(out_weight, "tm", axis=1, tiled=True),
        lax.all_gather(out_bias, "tm", axis=0, tiled=True),
        lax.all_gather(ln2_gain, "tm", axis=0, tiled=True),
        lax.all_gather(ln2_bias, "tm", axis=0, tiled=True),
        lax.all_gather(fc1_weight, "tm", axis=1, tiled=True),
        lax.all_gather(fc1_bias, "tm", axis=0, tiled=True),
        lax.all_gather(fc2_weight, "tm", axis=1, tiled=True),
        lax.all_gather(fc2_bias, "tm", axis=0, tiled=True),
    )
    tm_parts = lax.axis_size("tm")
    tm_place = lax.axis_index("tm")
    clip_count, frame_count, mel_count = mel_frames.shape
    state_dev = frame_count // 2
    model_width = conv2_weight.shape[2]
    all_states = state_dev * tm_parts
    score_scale = 1.0 / math.sqrt(HEAD_DIM)
    gain_one = ln1_gain.astype(jnp.float32)
    shift_one = ln1_bias.astype(jnp.float32)
    gain_two = ln2_gain.astype(jnp.float32)
    shift_two = ln2_bias.astype(jnp.float32)
    frame_ids = tm_place * frame_count + jnp.arange(frame_count)
    frame_valid = frame_ids[None, :] < lengths[:, None]
    masked_mel = jnp.where(frame_valid[:, :, None], mel_frames, jnp.zeros_like(mel_frames))
    mel_ext = with_halo(masked_mel, (("tm", 1),), 1)
    mel_taps = jnp.concatenate(
        [
            mel_ext[:, 0:frame_count],
            mel_ext[:, 1 : frame_count + 1],
            mel_ext[:, 2 : frame_count + 2],
        ],
        axis=2,
    )
    conv1_flat = conv1_weight.reshape(3 * mel_count, model_width)
    conv1_pre = jnp.einsum("cfk,ko->cfo", mel_taps, conv1_flat, preferred_element_type=jnp.float32)
    conv1_pre = conv1_pre + conv1_bias.astype(jnp.float32)
    frame_act = gelu_exact(conv1_pre).astype(jnp.bfloat16)
    left_edge = passed_along(frame_act[:, frame_count - 1 :], "tm", 1)
    frame_pairs = frame_act.reshape(clip_count, state_dev, 2, model_width)
    even_frames = frame_pairs[:, :, 0]
    odd_frames = frame_pairs[:, :, 1]
    before_frames = jnp.concatenate([left_edge, odd_frames[:, : state_dev - 1]], axis=1)
    state_taps = jnp.concatenate([before_frames, even_frames, odd_frames], axis=2)
    conv2_flat = conv2_weight.reshape(3 * model_width, model_width)
    conv2_pre = jnp.einsum(
        "csk,ko->cso", state_taps, conv2_flat, preferred_element_type=jnp.float32
    )
    conv2_pre = conv2_pre + conv2_bias.astype(jnp.float32)
    block_input = (
        gelu_exact(conv2_pre) + positions(tm_place * state_dev, state_dev, model_width)[None]
    )
    key_valid = 2 * jnp.arange(all_states)[None, :] < lengths[:, None]

    def project(inputs):
        normed = layer_norm(inputs, gain_one, shift_one).astype(jnp.bfloat16)
        mixed = jnp.einsum("csd,de->cse", normed, qkv_weight, preferred_element_type=jnp.float32)
        query_rows = (mixed[:, :, :model_width] + q_bias.astype(jnp.float32)).astype(jnp.bfloat16)
        key_rows = mixed[:, :, model_width : 2 * model_width].astype(jnp.bfloat16)
        value_rows = (mixed[:, :, 2 * model_width :] + v_bias.astype(jnp.float32)).astype(
            jnp.bfloat16
        )
        return (normed, query_rows, key_rows, value_rows)

    def score_rows(query_rows, key_whole):
        query_heads = query_rows.reshape(clip_count, state_dev, HEADS, HEAD_DIM)
        key_heads = key_whole.reshape(clip_count, all_states, HEADS, HEAD_DIM)
        scores = jnp.einsum(
            "cqhd,ckhd->chqk", query_heads, key_heads, preferred_element_type=jnp.float32
        )
        return jnp.where(key_valid[:, None, None, :], scores * score_scale, -1e30)

    normed1, queries, local_keys, local_values = project(block_input)
    keys_whole, values_whole = (
        lax.all_gather(local_keys, "tm", axis=1, tiled=True),
        lax.all_gather(local_values, "tm", axis=1, tiled=True),
    )
    scores = score_rows(queries, keys_whole)
    largest = jnp.max(scores, axis=-1, keepdims=True)
    exponent = jnp.exp(scores - largest)
    row_total = jnp.sum(exponent, axis=-1, keepdims=True)
    row_lse = largest + jnp.log(row_total)
    probs_low = (exponent / row_total).astype(jnp.bfloat16)
    value_heads = values_whole.reshape(clip_count, all_states, HEADS, HEAD_DIM)
    attended = jnp.einsum(
        "chqk,ckhd->cqhd", probs_low, value_heads, preferred_element_type=jnp.float32
    )
    attended = attended.reshape(clip_count, state_dev, model_width).astype(jnp.bfloat16)
    branch = jnp.einsum("csd,de->cse", attended, out_weight, preferred_element_type=jnp.float32)
    middle = block_input + branch + out_bias.astype(jnp.float32)
    normed2 = layer_norm(middle, gain_two, shift_two).astype(jnp.bfloat16)
    hidden_pre = jnp.einsum("csd,df->csf", normed2, fc1_weight, preferred_element_type=jnp.float32)
    hidden_pre = hidden_pre + fc1_bias.astype(jnp.float32)
    hidden_act = gelu_exact(hidden_pre).astype(jnp.bfloat16)
    mlp_out = jnp.einsum("csf,fd->csd", hidden_act, fc2_weight, preferred_element_type=jnp.float32)
    out_states = (middle + mlp_out + fc2_bias.astype(jnp.float32)).astype(jnp.bfloat16)
    cot_float = cotangent.astype(jnp.float32)
    fc2_weight_grad = jnp.einsum(
        "csf,csd->fd", hidden_act, cotangent, preferred_element_type=jnp.float32
    )
    fc2_bias_grad = jnp.sum(cot_float, axis=(0, 1))
    act_grad = jnp.einsum("csd,fd->csf", cotangent, fc2_weight, preferred_element_type=jnp.float32)
    hidden_grad = gelu_back(hidden_pre, act_grad).astype(jnp.bfloat16)
    fc1_weight_grad = jnp.einsum(
        "csd,csf->df", normed2, hidden_grad, preferred_element_type=jnp.float32
    )
    fc1_bias_grad = jnp.sum(hidden_grad.astype(jnp.float32), axis=(0, 1))
    normed2_grad = jnp.einsum(
        "csf,df->csd", hidden_grad, fc1_weight, preferred_element_type=jnp.float32
    )
    middle_part, ln2_gain_grad, ln2_bias_grad = jax.vjp(layer_norm, middle, gain_two, shift_two)[1](
        normed2_grad
    )
    middle_grad = cot_float + middle_part
    branch_grad = middle_grad.astype(jnp.bfloat16)
    out_weight_grad = jnp.einsum(
        "csi,csd->id", attended, branch_grad, preferred_element_type=jnp.float32
    )
    out_bias_grad = jnp.sum(branch_grad.astype(jnp.float32), axis=(0, 1))
    attended_flat = jnp.einsum(
        "csd,id->csi", branch_grad, out_weight, preferred_element_type=jnp.float32
    )
    attended_flat = attended_flat.astype(jnp.bfloat16)
    attended_grad = attended_flat.reshape(clip_count, state_dev, HEADS, HEAD_DIM)
    normed_again, queries_back, keys_again, values_again = project(block_input)
    keys_back, values_back = (
        lax.all_gather(keys_again, "tm", axis=1, tiled=True),
        lax.all_gather(values_again, "tm", axis=1, tiled=True),
    )
    back_scores = score_rows(queries_back, keys_back)
    attn_probs = jnp.exp(back_scores - row_lse)
    value_back = values_back.reshape(clip_count, all_states, HEADS, HEAD_DIM)
    key_back = keys_back.reshape(clip_count, all_states, HEADS, HEAD_DIM)
    query_back = queries_back.reshape(clip_count, state_dev, HEADS, HEAD_DIM)
    probs_grad = jnp.einsum(
        "cqhd,ckhd->chqk", attended_grad, value_back, preferred_element_type=jnp.float32
    )
    row_dot = jnp.sum(attn_probs * probs_grad, axis=-1, keepdims=True)
    score_grad = (attn_probs * (probs_grad - row_dot)).astype(jnp.bfloat16)
    queries_grad = jnp.einsum(
        "chqk,ckhd->cqhd", score_grad, key_back, preferred_element_type=jnp.float32
    )
    queries_grad = (
        (queries_grad * score_scale)
        .reshape(clip_count, state_dev, model_width)
        .astype(jnp.bfloat16)
    )
    probs_round = attn_probs.astype(jnp.bfloat16)
    values_term = jnp.einsum(
        "chqk,cqhd->ckhd", probs_round, attended_grad, preferred_element_type=jnp.float32
    )
    keys_term = jnp.einsum(
        "chqk,cqhd->ckhd", score_grad, query_back, preferred_element_type=jnp.float32
    )
    keys_term = keys_term * score_scale
    keys_sum, values_sum = (
        lax.psum_scatter(
            keys_term.reshape(clip_count, all_states, model_width).astype(jnp.bfloat16),
            "tm",
            scatter_dimension=1,
            tiled=True,
        ).astype(jnp.float32),
        lax.psum_scatter(
            values_term.reshape(clip_count, all_states, model_width).astype(jnp.bfloat16),
            "tm",
            scatter_dimension=1,
            tiled=True,
        ).astype(jnp.float32),
    )
    keys_grad = keys_sum.astype(jnp.bfloat16)
    values_grad = values_sum.astype(jnp.bfloat16)
    projected_grad = jnp.concatenate([queries_grad, keys_grad, values_grad], axis=2)
    qkv_weight_grad = jnp.einsum(
        "csd,cse->de", normed1, projected_grad, preferred_element_type=jnp.float32
    )
    q_bias_grad = jnp.sum(queries_grad.astype(jnp.float32), axis=(0, 1))
    v_bias_grad = jnp.sum(values_grad.astype(jnp.float32), axis=(0, 1))
    normed1_grad = jnp.einsum(
        "cse,de->csd", projected_grad, qkv_weight, preferred_element_type=jnp.float32
    )
    input_part, ln1_gain_grad, ln1_bias_grad = jax.vjp(
        layer_norm, block_input, gain_one, shift_one
    )[1](normed1_grad)
    input_grad = middle_grad + input_part
    conv2_grad = gelu_back(conv2_pre, input_grad).astype(jnp.bfloat16)
    conv2_weight_grad = jnp.einsum(
        "csk,cso->ko", state_taps, conv2_grad, preferred_element_type=jnp.float32
    )
    conv2_weight_grad = conv2_weight_grad.reshape(3, model_width, model_width)
    conv2_bias_grad = jnp.sum(conv2_grad.astype(jnp.float32), axis=(0, 1))
    taps_grad = jnp.einsum(
        "cso,ko->csk", conv2_grad, conv2_flat, preferred_element_type=jnp.float32
    )
    before_grad = taps_grad[:, :, :model_width]
    even_grad = taps_grad[:, :, model_width : 2 * model_width]
    odd_grad = taps_grad[:, :, 2 * model_width :]
    edge_back = passed_along(before_grad[:, :1], "tm", -1)
    odd_total = odd_grad + jnp.concatenate([before_grad[:, 1:], edge_back], axis=1)
    frame_grad = jnp.stack([even_grad, odd_total], axis=2).reshape(
        clip_count, frame_count, model_width
    )
    conv1_grad = gelu_back(conv1_pre, frame_grad).astype(jnp.bfloat16)
    conv1_weight_grad = jnp.einsum(
        "cfk,cfo->ko", mel_taps, conv1_grad, preferred_element_type=jnp.float32
    )
    conv1_weight_grad = conv1_weight_grad.reshape(3, mel_count, model_width)
    conv1_bias_grad = jnp.sum(conv1_grad.astype(jnp.float32), axis=(0, 1))
    mel_taps_grad = jnp.einsum(
        "cfo,ko->cfk", conv1_grad, conv1_flat, preferred_element_type=jnp.float32
    )
    ext_grad = (
        jnp.pad(mel_taps_grad[:, :, :mel_count], ((0, 0), (0, 2), (0, 0)))
        + jnp.pad(mel_taps_grad[:, :, mel_count : 2 * mel_count], ((0, 0), (1, 1), (0, 0)))
        + jnp.pad(mel_taps_grad[:, :, 2 * mel_count :], ((0, 0), (2, 0), (0, 0)))
    )
    rim_terms = jnp.stack([ext_grad[:, 0], ext_grad[:, frame_count + 1]], axis=1)
    rims_ext = with_halo(rim_terms, (("tm", 1),), 1)
    mel_inner = ext_grad[:, 1 : frame_count + 1]
    mel_inner = mel_inner.at[:, 0].add(rims_ext[:, 0]).at[:, frame_count - 1].add(rims_ext[:, 3])
    mel_grad = jnp.where(frame_valid[:, :, None], mel_inner, 0.0).astype(jnp.bfloat16)
    grads_list = (
        conv1_weight_grad,
        conv1_bias_grad,
        conv2_weight_grad,
        conv2_bias_grad,
        ln1_gain_grad,
        ln1_bias_grad,
        qkv_weight_grad,
        q_bias_grad,
        v_bias_grad,
        out_weight_grad,
        out_bias_grad,
        ln2_gain_grad,
        ln2_bias_grad,
        fc1_weight_grad,
        fc1_bias_grad,
        fc2_weight_grad,
        fc2_bias_grad,
    )
    pieces = []
    rotated_shapes = []
    for member, split_axis in zip(grads_list, split_axes):
        rotated = jnp.moveaxis(member, split_axis, 0)
        rotated_shapes.append(rotated.shape)
        pieces.append(rotated.reshape(tm_parts, -1))
    packed = jnp.concatenate(pieces, axis=1)
    clip_parts = lax.axis_size("clip")
    width_share = packed.shape[1] // clip_parts
    arranged = packed.reshape(tm_parts, clip_parts, width_share).transpose(1, 0, 2)
    arranged = arranged.reshape(clip_parts * tm_parts, width_share)
    summed_share = lax.psum_scatter(arranged, ("clip", "tm"), scatter_dimension=0, tiled=True)
    owned_flat = (
        lax.all_gather(summed_share.astype(jnp.bfloat16), "clip", axis=0, tiled=True)
        .astype(summed_share.dtype)
        .reshape(-1)
    )
    offset = 0
    results = []
    for rotated_shape, split_axis in zip(rotated_shapes, split_axes):
        local_shape = (rotated_shape[0] // tm_parts,) + tuple(rotated_shape[1:])
        entry_count = math.prod(local_shape)
        segment = owned_flat[offset : offset + entry_count].reshape(local_shape)
        results.append(jnp.moveaxis(segment, 0, split_axis))
        offset = offset + entry_count
    return (out_states, mel_grad) + tuple(results)


def solution(mesh):
    return jax.shard_map(
        per_device,
        mesh=mesh,
        in_specs=(
            P("clip", "tm", None),
            P("clip"),
            P(None, None, "tm"),
            P("tm"),
            P(None, None, "tm"),
            P("tm"),
            P("tm"),
            P("tm"),
            P(None, "tm"),
            P("tm"),
            P("tm"),
            P(None, "tm"),
            P("tm"),
            P("tm"),
            P("tm"),
            P(None, "tm"),
            P("tm"),
            P(None, "tm"),
            P("tm"),
            P("clip", "tm", None),
        ),
        out_specs=(
            P("clip", "tm", None),
            P("clip", "tm", None),
            P(None, None, "tm"),
            P("tm"),
            P(None, None, "tm"),
            P("tm"),
            P("tm"),
            P("tm"),
            P(None, "tm"),
            P("tm"),
            P("tm"),
            P(None, "tm"),
            P("tm"),
            P("tm"),
            P("tm"),
            P(None, "tm"),
            P("tm"),
            P(None, "tm"),
            P("tm"),
        ),
        check_vma=False,
    )
```

profile of v0, /device:TPU:0, one launch (start us, length us, event | category | flops | bytes accessed | tf_op | source)
XLA Modules:
  0.0 1736.0 jit_solution(3783372368277894222)
XLA Ops:
  24.5 14.6 all-reduce.14
  40.8 8.7 all_gather.62
  52.5 10.2 multiply_convert_fusion.3
  74.7 5.3 fusion.58
  98.3 5.3 all-gather
  104.9 17.2 all-gather.17.cloned.1.call-done
  125.2 12.4 fusion.6
  137.6 11.3 fusion
  152.6 4.7 copy.91
  157.3 13.5 fusion.49
  175.9 34.5 %all-gather.21.cloned.1.call-done = bf16[768,3072]{1,0:T(8,128)(2,1)} async-done(((bf16[768,768]{1,0:T(8,128)(2,1)}), bf16[768,3072]{1,0:T(8,128)(2,1)}) %all-gather.21.cloned.1.call-update) | async-done | bytes 4718608 | tf_op jit(solution)/shard_map/all_gather | solution.py:107
  210.4 7.4 fusion.46
  220.8 15.9 multiply_convert_fusion.2
  236.7 12.8 all-gather.23.cloned.1.call-done
  249.5 10.9 convert_reduce_fusion.1
  260.4 6.4 multiply_reduce_fusion.1
  273.8 12.3 fusion.33
  290.9 20.3 %multiply_reduce_fusion = (f32[2,12,256]{2,1,0:T(8,128)S(1)}, f32[2,12,256,1024]{3,2,1,0:T(8,128)}) fusion(f32[2,12,256]{2,1,0:T(8,128)S(1)} %log_add_fusion, f32[2,12,256,1024]{3,2,1,0:T(8,128)} %get-tuple-element.149, pred[2,1024]{1,0:T(4,128)(4,1)S(1)} %broadcast_compare_fusion, bf16[2,256,12,64]{1,3,2,0:T(8,128)(2,1)} %bitcast.144, ...), kind=kOutput, calls=%fused_computation.2 | convolution fusion | flops 836757504 | bytes 54315008 | tf_op jit(solution)/shard_map/cqhd,ckhd->chqk/dot_general | solution.py:235
  311.2 17.0 multiply_convert_fusion
  333.6 4.7 copy.96
  338.6 9.4 convert_reduce_fusion.6
  354.5 9.3 convolution_bitcast_fusion.2
  363.8 12.4 reshape.400
  376.2 8.2 convolution_bitcast_fusion.1
  384.4 9.6 copy.108
  394.0 13.9 reshape.402
  414.5 5.2 convert_reduce_fusion.7
  423.4 5.7 fusion.56
  429.0 5.0 convolution_bitcast_fusion
  434.3 11.0 copy.102
  445.4 12.6 reshape.389
  458.2 9.4 reshape.393
  476.4 5.3 convert_reduce_fusion.2
  487.8 37.7 %dynamic-update-slice.18 = f32[4,2260608]{1,0:T(4,128)} dynamic-update-slice(f32[4,2260608]{1,0:T(4,128)} %dynamic-update-slice.17, f32[4,442368]{1,0:T(4,128)} %reshape.389, s32[]{} %constant.291, s32[]{} %constant.293) | dynamic-update-slice | bytes 14155780
  529.8 6.6 constant_dynamic-update-slice_fusion.1
  544.5 49.6 %dynamic-update-slice.29 = f32[4,2260608]{1,0:T(4,128)} dynamic-update-slice(f32[4,2260608]{1,0:T(4,128)} %dynamic-update-slice.28, f32[4,589824]{1,0:T(4,128)} %reshape.400, s32[]{} %constant.291, s32[]{} %constant.304) | dynamic-update-slice | bytes 18874372
  595.7 49.3 %dynamic-update-slice.31 = f32[4,2260608]{1,0:T(4,128)} dynamic-update-slice(f32[4,2260608]{1,0:T(4,128)} %dynamic-update-slice.30, f32[4,589824]{1,0:T(4,128)} %reshape.402, s32[]{} %constant.291, s32[]{} %constant.306) | dynamic-update-slice | bytes 18874372
  646.4 102.5 %reshape.488 = f32[9042432]{0:T(1024)} reshape(f32[4,2260608]{1,0:T(4,128)} %dynamic-update-slice.32) | data formatting | bytes 72339456
  748.9 45.1 %reshape.404 = f32[4,8,282576]{2,1,0:T(8,128)} reshape(f32[9042432]{0:T(1024)} %reshape.488) | data formatting | bytes 72339456 | tf_op jit(solution)/shard_map/reshape | solution.py:349
  794.0 31.5 %copy.125 = f32[4,8,282576]{2,0,1:T(4,128)} copy(f32[4,8,282576]{2,1,0:T(8,128)} %reshape.404) | data formatting | bytes 72339456 | tf_op jit(solution)/shard_map/reshape | solution.py:349
  825.5 40.8 %reshape.405 = f32[32,282576]{1,0:T(8,128)} reshape(f32[8,4,282576]{2,1,0:T(4,128)} %bitcast.124) | data formatting | bytes 72339456 | tf_op jit(solution)/shard_map/reshape | solution.py:350
  866.2 586.3 %all-reduce.16 = bf16[32,282576]{1,0:T(8,128)(2,1)} all-reduce(f32[32,282576]{1,0:T(8,128)} %reshape.405), channel_id=4, replica_groups=mesh['clip'=8,'tm'=4] {'clip','tm'}, use_global_device_ids=true, to_apply=%region_24.25.clone | all-reduce | flops 9042432 | bytes 54254592
  1452.6 4.7 fusion.52
  1457.4 6.9 add_convert_fusion.3
  1472.7 116.7 %all-gather.25.cloned.1.call-done = bf16[8,1,282576]{2,1,0:T(2,128)(2,1)} async-done(((bf16[1,1,282576]{2,1,0:T(2,128)(2,1)}), bf16[8,1,282576]{2,1,0:T(2,128)(2,1)}) %all-gather.25.cloned.1.call-update) | async-done | bytes 4521232 | tf_op jit(solution)/shard_map/all_gather | solution.py:353
  1589.5 97.2 %convert_reduce_fusion = f32[8,282576]{1,0:T(8,128)} fusion(bf16[8,1,282576]{2,1,0:T(2,128)(2,1)} %all-gather.25.cloned.1.call-done), kind=kLoop, calls=%fused_computation.14 | loop fusion | flops 2260608 | bytes 13563648 | tf_op jit(solution)/shard_map/reshape | solution.py:355
  1686.6 11.8 reshape.415
  1705.8 5.9 fusion.83
  (310 shorter events, 164.9 us)
Async XLA Ops:
  7.2 63.2 %all-gather.11.cloned.1.call-start = ((), (), s32[]{:S(2)}) async-start(), calls=%async_computation.2 | async-start | bytes 4423680 | tf_op jit(solution)/shard_map/all_gather | solution.py:96
  7.9 77.7 %all-gather.13.cloned.1.call-start = ((), (), s32[]{:S(2)}) async-start(), calls=%async_computation.3 | async-start | bytes 4423680 | tf_op jit(solution)/shard_map/all_gather | solution.py:100
  9.7 53.1 %copy-start.32 = (bf16[2,512,80]{1,2,0:T(8,128)(2,1)}, bf16[2,512,80]{1,2,0:T(8,128)(2,1)S(1)}, u32[]{:S(2)}) copy-start(bf16[2,512,80]{1,2,0:T(8,128)(2,1)S(1)} %broadcast_select_fusion) | copy-start | bytes 491524
  9.8 42.7 %collective-permute-start.1 = (bf16[2,1,80]{1,2,0:T(8,128)(2,1)S(1)}, bf16[2,1,80]{1,2,0:T(8,128)(2,1)S(1)}, u32[]{:S(2)}, u32[]{:S(2)}) collective-permute-start(bf16[2,1,80]{1,2,0:T(8,128)(2,1)S(1)} %get-tuple-element.143), channel_id=1, source_target_pairs={{1,0},{2,1},{3,2},{5,4},{6,5},{7,6},{9,8},{10,9},{11,10},{13,12},{... | collective-permute-start | bytes 968 | tf_op jit(solution)/shard_map/ppermute | solution.py:20
  11.1 41.4 %collective-permute-start = (bf16[2,1,80]{1,2,0:T(8,128)(2,1)S(1)}, bf16[2,1,80]{1,2,0:T(8,128)(2,1)S(1)}, u32[]{:S(2)}, u32[]{:S(2)}) collective-permute-start(bf16[2,1,80]{1,2,0:T(8,128)(2,1)S(1)} %get-tuple-element.142), channel_id=1, source_target_pairs={{0,1},{1,2},{2,3},{4,5},{5,6},{6,7},{8,9},{9,10},{10,11},{12,13},{... | collective-permute-start | bytes 968 | tf_op jit(solution)/shard_map/ppermute | solution.py:19
  14.1 107.9 %all-gather.17.cloned.1.call-start = ((), (), s32[]{:S(2)}) async-start(), calls=%async_computation.5 | async-start | bytes 3932160 | tf_op jit(solution)/shard_map/all_gather | solution.py:175
  51.9 10.9 copy-start.44
  52.4 10.3 copy-start.23
  52.4 33.2 %copy-start.46 = (f32[768]{0:T(1024)}, f32[768]{0:T(1024)S(1)}, u32[]{:S(2)}) copy-start(f32[768]{0:T(1024)S(1)} %convert_element_type.175) | copy-start | bytes 9220
  52.4 33.2 %copy-start.34 = (f32[768]{0:T(1024)}, f32[768]{0:T(1024)S(1)}, u32[]{:S(2)}) copy-start(f32[768]{0:T(1024)S(1)} %convert_element_type.174) | copy-start | bytes 9220
  52.5 10.3 copy-start.58
  52.5 10.3 copy-start.60
  63.4 11.3 collective-permute-start.2
  74.7 6.5 copy-start.21
  85.6 7.5 copy-start.53
  85.6 7.5 copy-start.52
  93.0 59.5 %all-gather.15.cloned.1.call-start = ((), (), s32[]{:S(2)}) async-start(), calls=%async_computation.4 | async-start | bytes 3932160 | tf_op jit(solution)/shard_map/all_gather | solution.py:176
  93.2 10.5 copy-start.50
  93.2 10.5 copy-start.49
  96.2 75.3 %all-gather.19.cloned.1.call-start = ((), (), s32[]{:S(2)}) async-start(), calls=%async_computation.6 | async-start | bytes 1474560 | tf_op jit(solution)/shard_map/all_gather | solution.py:103
  96.8 113.6 %all-gather.21.cloned.1.call-start = ((), (), s32[]{:S(2)}) async-start(), calls=%async_computation.7 | async-start | bytes 5898240 | tf_op jit(solution)/shard_map/all_gather | solution.py:107
  97.4 152.1 %all-gather.23.cloned.1.call-start = ((), (), s32[]{:S(2)}) async-start(), calls=%async_computation.8 | async-start | bytes 5898240 | tf_op jit(solution)/shard_map/all_gather | solution.py:109
  98.1 309.8 %reduce-scatter.5.cloned.1.call-start = ((), (), s32[]{:S(2)}) async-start(), calls=%async_computation.10 | async-start | bytes 3932160 | tf_op jit(solution)/shard_map/reduce_scatter | solution.py:263
  249.5 10.9 copy-start.13
  260.4 6.4 copy-start.62
  290.8 117.1 %reduce-scatter.3.cloned.1.call-start = ((), (), s32[]{:S(2)}) async-start(), calls=%async_computation.9 | async-start | bytes 3932160 | tf_op jit(solution)/shard_map/reduce_scatter | solution.py:257
  311.1 17.0 copy-start.5
  338.4 1251.1 %all-gather.25.cloned.1.call-start = ((), (), s32[]{:S(2)}) async-start(), calls=%async_computation.11 | async-start | bytes 10174464 | tf_op jit(solution)/shard_map/all_gather | solution.py:353
  363.8 12.4 copy-start.20
  394.0 13.9 copy-start.2
  394.0 13.9 copy-start.35
  394.0 13.9 copy-start.37
  421.7 12.5 copy-start.15
  421.8 7.3 copy-start.27
  421.8 7.3 copy-start.47
  421.8 7.3 copy-start.57
  421.8 46.0 %collective-permute-start.3 = (f32[2,1,768]{2,1,0:T(1,128)S(1)}, f32[2,1,768]{2,1,0:T(1,128)S(1)}, u32[]{:S(2)}, u32[]{:S(2)}) collective-permute-start(f32[2,1,768]{2,1,0:T(1,128)S(1)} %slice.220), channel_id=1, source_target_pairs={{1,0},{2,1},{3,2},{5,4},{6,5},{7,6},{9,8},{10,9},{11,10},{13,12},{... | collective-permute-start | bytes 18440 | tf_op jit(solution)/shard_map/ppermute | solution.py:28
  476.4 6.4 copy-start.59
  476.4 6.4 copy-start.61
  529.7 9.3 copy-start.6
  1457.3 7.0 copy-start.11
  1457.4 7.0 copy-start.24
  1464.9 7.1 copy-start.39
  1465.1 3.0 collective-permute-start.4
  1466.9 4.7 collective-permute-start.5
  1699.8 11.8 slice-start
  1699.8 11.8 slice-start.1
  1705.8 6.6 slice-start.3
  (35 other events, 133.8 us)
Sparse Core Ops, SparseCore 0:
  9.6 34.0 all-gather.10
  45.2 30.7 all-gather.12
  93.2 28.8 all-gather.16
  124.0 28.5 all-gather.14
  154.0 17.4 all-gather.18
  172.9 37.4 all-gather.20
  212.0 37.4 all-gather.22
  290.9 37.9 reduce-scatter.4
  338.5 37.8 reduce-scatter.2
  1457.4 131.9 all-gather.24
where the time goes:
time: 1750 us; the launch traced here: 1740 us
  blocking collectives  615 us (35%)
  local copies, waits for them, and re-layouts  565 us (32%)
  waiting for transfers between devices  191 us (11%)
  other arithmetic  170 us (10%)
  matrix products  167 us (10%)
    unnamed x2, blocking collectives  601 us
    unnamed x176, local copies, waits for them, and re-layouts  294 us
    all_gather x1, waiting for transfers between devices, per_device(): lax.all_gather(summed_share.astype(jnp.bfloat16), 'clip', axis=0, tiled=T...  117 us
    reshape x1, other arithmetic, per_device(): owned_flat = lax.all_gather(summed_share.astype(jnp.bfloat16), 'clip', ax...  97.2 us
    reshape x2, local copies, waits for them, and re-layouts, per_device(): packed.reshape(tm_parts, clip_parts, width_share).transpose(1, 0, 2)  76.6 us
    reshape x17, local copies, waits for them, and re-layouts, per_device(): pieces.append(rotated.reshape(tm_parts, -1))  53 us
    reshape x1, local copies, waits for them, and re-layouts, per_device(): arranged = arranged.reshape(clip_parts * tm_parts, width_share)  40.8 us
  transfers between devices with their start and end apart: 16, of which 7 were waited for; matrix products, arithmetic and copies ran while one was open for 17% of the time, Pallas kernels for 0%

commit v1 on v0

v1 whole, which is shorter than its diff:
```python
import math

import jax
import jax.numpy as jnp
from jax import lax
from jax.sharding import PartitionSpec as P

HEADS = 12
HEAD_DIM = 64
F32 = jnp.float32
BF16 = jnp.bfloat16
SCALE = 1.0 / math.sqrt(HEAD_DIM)
ROWS = 16


def xor_swap(array, axis, mask):
    size = lax.axis_size(axis)
    return lax.ppermute(array, axis, [(i, i ^ mask) for i in range(size)])


def pick(array, index, axis=0):
    return lax.dynamic_index_in_dim(array, index, axis=axis, keepdims=False)


def bits_of(size):
    return [1 << b for b in range(size.bit_length() - 1)]


def gelu_pair(v):
    a = jnp.abs(v) * (1.0 / math.sqrt(2.0))
    t = 1.0 / (1.0 + 0.3275911 * a)
    poly = t * (
        0.254829592
        + t * (-0.284496736 + t * (1.421413741 + t * (-1.453152027 + t * 1.061405429)))
    )
    bell = jnp.exp(-0.5 * v * v)
    tail = 0.5 * poly * bell
    cdf = jnp.where(v >= 0, 1.0 - tail, tail)
    return v * cdf, cdf + v * bell * (1.0 / math.sqrt(2.0 * math.pi))


def norm_parts(v):
    center = v - jnp.mean(v, axis=-1, keepdims=True)
    spread = jnp.mean(center * center, axis=-1, keepdims=True)
    scale = lax.rsqrt(spread + 1e-05)
    return center * scale, scale


def norm_back(grad, unit, scale, gain):
    a = grad * gain
    mean_a = jnp.mean(a, axis=-1, keepdims=True)
    mean_an = jnp.mean(a * unit, axis=-1, keepdims=True)
    return (a - mean_a - unit * mean_an) * scale


def positions(starts, count, width):
    half = width // 2
    rates = jnp.exp(-(math.log(10000.0) / (half - 1)) * jnp.arange(half, dtype=F32))
    angles = (starts[:, None] + jnp.arange(count)[None, :]).astype(F32)[..., None] * rates
    return jnp.concatenate([jnp.sin(angles), jnp.cos(angles)], axis=-1)


def mat(a, b):
    return jnp.dot(a, b, preferred_element_type=F32)


def mat_t(a, b):
    return lax.dot_general(a, b, (((1,), (1,)), ((), ())), preferred_element_type=F32)


def gather_rows(shard, place, parts):
    pieces = [shard]
    masks = [0]
    for mask in [m for m in bits_of(parts) if m > 1]:
        pieces = pieces + [xor_swap(p, "tm", mask) for p in pieces]
        masks = masks + [m ^ mask for m in masks]
    stack = jnp.stack(pieces)
    other = xor_swap(stack, "tm", 1)
    whole = jnp.zeros((parts,) + shard.shape, shard.dtype)
    for i, mask in enumerate(masks):
        whole = lax.dynamic_update_slice(whole, stack[i][None], (place ^ mask, 0, 0))
        whole = lax.dynamic_update_slice(whole, other[i][None], (place ^ mask ^ 1, 0, 0))
    return whole.reshape(parts * shard.shape[0], shard.shape[1])


def halve(array, axis, index, shift, size):
    for bit in bits_of(size):
        blocks = array.reshape((array.shape[0] // 2, 2) + array.shape[1:])
        mine = (index // bit) % 2
        got = xor_swap(pick(blocks, 1 - mine, 1), axis, bit * shift)
        array = (pick(blocks, mine, 1).astype(F32) + got.astype(F32)).astype(array.dtype)
    return array


def double(array, axis, index, shift, size):
    for bit in reversed(bits_of(size)):
        mine = (index // bit) % 2
        got = xor_swap(array, axis, bit * shift)
        array = jnp.stack(
            [jnp.where(mine == 0, array, got), jnp.where(mine == 0, got, array)], axis=1
        )
        array = array.reshape((array.shape[0] * 2,) + array.shape[2:])
    return array


def per_device(
    mel_frames,
    lengths,
    conv1_weight,
    conv1_bias,
    conv2_weight,
    conv2_bias,
    ln1_gain,
    ln1_bias,
    qkv_weight,
    q_bias,
    v_bias,
    out_weight,
    out_bias,
    ln2_gain,
    ln2_bias,
    fc1_weight,
    fc1_bias,
    fc2_weight,
    fc2_bias,
    cotangent,
):
    parts = lax.axis_size("tm")
    place = lax.axis_index("tm")
    clips = lax.axis_size("clip")
    clip_place = lax.axis_index("clip")
    y_size = parts // 2
    x_size = y_size
    z_size = clips // x_size
    core, y_place = place % 2, place // 2
    x_place, z_place = clip_place % x_size, clip_place // x_size
    mine = y_place % 2
    frames, mels = mel_frames.shape[1:]
    states, width = cotangent.shape[1:]
    hidden = fc1_weight.shape[1] * parts
    rows = 2 * states

    w1_own = jnp.pad(conv1_weight.reshape(3 * mels, -1).T, ((0, 0), (0, 16)))
    w2_own = conv2_weight.reshape(3 * width, -1).T
    vec_own = jnp.concatenate(
        [
            conv1_bias,
            conv2_bias,
            ln1_gain,
            ln1_bias,
            q_bias,
            v_bias,
            out_bias,
            ln2_gain,
            ln2_bias,
            fc2_bias,
            fc1_bias,
        ]
    )
    vec_own = jnp.pad(vec_own, (0, -vec_own.shape[0] % 128)).reshape(-1, 128)
    w1 = gather_rows(w1_own, place, parts)
    vecs = gather_rows(vec_own, place, parts)
    w2 = gather_rows(w2_own, place, parts)
    wqkv = gather_rows(qkv_weight.T, place, parts)
    wout = gather_rows(out_weight.T, place, parts)
    wfc1 = gather_rows(fc1_weight.T, place, parts)
    wfc2 = gather_rows(fc2_weight.T, place, parts)
    share = conv1_bias.shape[0]
    vecs = vecs.reshape(parts, -1).astype(F32)
    b1, b2, gain_one, shift_one, bq, bv, bout, gain_two, shift_two, bfc2 = [
        vecs[:, i * share : (i + 1) * share].reshape(-1) for i in range(10)
    ]
    bfc1 = vecs[:, 10 * share : 10 * share + fc1_bias.shape[0]].reshape(-1)

    def swapped(array):
        got = xor_swap(pick(array, 1 - mine), "tm", 2)
        own = pick(array, mine)
        return jnp.where(mine == 0, jnp.stack([own, got]), jnp.stack([got, own]))

    length = pick(lengths, mine)
    segs_of = lambda device: 4 * (device // 4) + 2 * jnp.arange(2) + device % 2
    seg = segs_of(place)
    frame_ids = seg[:, None] * frames + jnp.arange(frames)[None, :]
    frame_valid = (frame_ids < length)[..., None]
    mel_clip = swapped(mel_frames)
    cot = swapped(cotangent).reshape(rows, width)
    masked = jnp.where(frame_valid, mel_clip, jnp.zeros_like(mel_clip))
    pairs = masked.reshape(2, states, 2, mels)
    even, odd = pairs[:, :, 0], pairs[:, :, 1]

    def neighbours(first, last):
        got_first, got_last = xor_swap((first, last), "tm", 1)
        far_last, far_first = jnp.zeros_like(last[0]), jnp.zeros_like(first[0])
        if y_size > 2:
            up = [(i, i + 3) for i in range(parts - 3) if i % 2 == 1]
            far_last = lax.ppermute(last[1], "tm", up)
            far_first = lax.ppermute(first[0], "tm", [(j, i) for i, j in up])
        is_zero = core == 0
        before = jnp.stack(
            [
                jnp.where(is_zero, far_last, got_last[0]),
                jnp.where(is_zero, got_last[0], got_last[1]),
            ]
        )
        after = jnp.stack(
            [
                jnp.where(is_zero, got_first[0], got_first[1]),
                jnp.where(is_zero, got_first[1], far_first),
            ]
        )
        return before, after

    before, after = neighbours(even[:, 0], jnp.stack([even[:, -1], odd[:, -1]], axis=1))
    odd_before = jnp.concatenate([before[:, 1:2], odd[:, :-1]], axis=1)
    even_after = jnp.concatenate([even[:, 1:], after[:, None]], axis=1)
    taps = jnp.concatenate(
        [
            jnp.concatenate([odd_before, even, odd], axis=2).reshape(rows, 3 * mels),
            jnp.concatenate([even, odd, even_after], axis=2).reshape(rows, 3 * mels),
            jnp.concatenate([before[:, 0], before[:, 1], even[:, 0]], axis=1),
            jnp.zeros((ROWS - 2, 3 * mels), BF16),
        ],
        axis=0,
    )
    taps = jnp.pad(taps, ((0, 0), (0, 16)))
    frame_pre = mat_t(taps, w1) + b1
    frame_act, frame_slope = gelu_pair(frame_pre)
    frame_act = frame_act.astype(BF16)
    frame_slope = frame_slope.astype(BF16)
    even_act = frame_act[:rows]
    odd_act = frame_act[rows : 2 * rows]
    inside = (seg > 0)[:, None]
    edge_act = jnp.where(inside, frame_act[2 * rows : 2 * rows + 2], 0)
    edge_slope = jnp.where(inside, frame_slope[2 * rows : 2 * rows + 2], 0)
    prev_act = jnp.concatenate(
        [edge_act[:, None], odd_act.reshape(2, states, width)[:, :-1]], axis=1
    ).reshape(rows, width)
    state_taps = jnp.concatenate([prev_act, even_act, odd_act], axis=1)
    state_pre = mat_t(state_taps, w2) + b2
    state_act, state_slope = gelu_pair(state_pre)
    block_input = state_act + positions(seg * states, states, width).reshape(rows, width)
    unit1, scale1 = norm_parts(block_input)
    normed1 = (unit1 * gain_one + shift_one).astype(BF16)
    bias_qkv = jnp.concatenate([bq, jnp.zeros_like(bq), bv])
    mixed = (mat_t(normed1, wqkv) + bias_qkv).astype(BF16)
    queries = mixed[:, :width]
    keys = mixed[:, width : 2 * width]
    values = mixed[:, 2 * width :]

    group = [m for m in bits_of(parts) if m != 2]
    pair = jnp.stack([keys, values])
    masks = [0]
    for mask in group:
        pair = jnp.concatenate([pair, xor_swap(pair, "tm", mask)], axis=1)
        masks = masks + [m ^ mask for m in masks]
    segs = jnp.concatenate([segs_of(place ^ m) for m in masks])
    key_ids = (segs[:, None] * states + jnp.arange(states)[None, :]).reshape(-1)
    key_valid = 2 * key_ids < length
    all_states = key_ids.shape[0]

    def heads(array):
        return array.reshape(-1, HEADS, HEAD_DIM)

    q_h, k_h, v_h = heads(queries), heads(pair[0]), heads(pair[1])
    scores = jnp.einsum("qhd,khd->hqk", q_h, k_h, preferred_element_type=F32) * SCALE
    scores = jnp.where(key_valid, scores, -1e30)
    largest = jnp.max(scores, axis=-1, keepdims=True)
    exponent = jnp.exp(scores - largest)
    probs = (exponent / jnp.sum(exponent, axis=-1, keepdims=True)).astype(BF16)
    attended = jnp.einsum("hqk,khd->qhd", probs, v_h, preferred_element_type=F32)
    attended = attended.reshape(rows, width).astype(BF16)
    middle = block_input + mat_t(attended, wout) + bout
    unit2, scale2 = norm_parts(middle)
    normed2 = (unit2 * gain_two + shift_two).astype(BF16)
    hidden_act, hidden_slope = gelu_pair(mat_t(normed2, wfc1) + bfc1)
    hidden_act = hidden_act.astype(BF16)
    hidden_slope = hidden_slope.astype(BF16)
    out_rows = (middle + mat_t(hidden_act, wfc2) + bfc2).astype(BF16)

    def unswapped(array):
        got = xor_swap(pick(array, 1 - mine), "tm", 2)
        own = pick(array, mine)
        return jnp.where(mine == 0, jnp.stack([own, got]), jnp.stack([got, own]))

    out_states = unswapped(out_rows.reshape(2, states, width))

    def chip_grad(grad, acts):
        blocks = grad.reshape(rows, y_size, 2, -1)
        sent, kept = pick(blocks, 1 - core, 2), pick(blocks, core, 2)
        product = lambda g: jnp.einsum("ryn,rk->ynk", g, acts, preferred_element_type=F32)
        got = xor_swap(product(sent).astype(BF16), "tm", 1)
        total = (product(kept) + got.astype(F32)).astype(BF16)
        return total.reshape(y_size, -1, width)

    def all_sum(pieces):
        packed = jnp.concatenate(pieces, axis=1)
        sizes = [p.shape[1] for p in pieces]
        count = sum(sizes)
        step = ROWS * x_size * z_size
        packed = jnp.pad(packed, ((0, 0), (0, -count % step), (0, 0)))
        packed = halve(packed, "tm", y_place, 2, y_size)[0]
        packed = packed.reshape(z_size, x_size, -1, width).swapaxes(0, 1)
        packed = halve(packed, "clip", x_place, 1, x_size)[0]
        packed = halve(packed, "clip", z_place, x_size, z_size)
        packed = double(packed, "clip", z_place, x_size, z_size)
        packed = double(packed[None], "clip", x_place, 1, x_size)
        packed = packed.swapaxes(0, 1).reshape(-1, width)
        ends = [sum(sizes[: i + 1]) for i in range(len(sizes))]
        return [packed[e - s : e].astype(F32) for e, s in zip(ends, sizes)]

    cot_float = cot.astype(F32)
    fc2_part = chip_grad(cot, hidden_act)
    bfc2_grad = jnp.sum(cot_float, axis=0)
    hidden_grad = (mat(cot, wfc2) * hidden_slope.astype(F32)).astype(BF16)
    fc1_part = chip_grad(hidden_grad, normed2)
    bfc1_grad = jnp.sum(hidden_grad.astype(F32), axis=0)
    normed2_grad = mat(hidden_grad, wfc1)
    gain_two_grad = jnp.sum(normed2_grad * unit2, axis=0)
    shift_two_grad = jnp.sum(normed2_grad, axis=0)
    middle_grad = cot_float + norm_back(normed2_grad, unit2, scale2, gain_two)
    branch_grad = middle_grad.astype(BF16)
    out_part = chip_grad(branch_grad, attended)
    bout_grad = jnp.sum(branch_grad.astype(F32), axis=0)
    fc2_sum, fc1_sum, out_sum = all_sum([fc2_part, fc1_part, out_part])

    attended_grad = mat(branch_grad, wout).astype(BF16)
    a_h = heads(attended_grad)
    row_dot = jnp.sum(a_h.astype(F32) * heads(attended).astype(F32), axis=-1)
    probs_grad = jnp.einsum("qhd,khd->hqk", a_h, v_h, preferred_element_type=F32)
    score_grad = (probs.astype(F32) * (probs_grad - row_dot.T[..., None])).astype(BF16)
    queries_grad = jnp.einsum("hqk,khd->qhd", score_grad, k_h, preferred_element_type=F32)
    queries_grad = (queries_grad * SCALE).reshape(rows, width).astype(BF16)
    keys_term = jnp.einsum("hqk,qhd->khd", score_grad, q_h, preferred_element_type=F32) * SCALE
    values_term = jnp.einsum("hqk,qhd->khd", probs, a_h, preferred_element_type=F32)
    terms = jnp.stack(
        [keys_term.reshape(all_states, width), values_term.reshape(all_states, width)]
    ).astype(BF16)
    for mask in reversed(group):
        half = terms.shape[1] // 2
        got = xor_swap(terms[:, half:], "tm", mask)
        terms = (terms[:, :half].astype(F32) + got.astype(F32)).astype(BF16)
    projected_grad = jnp.concatenate([queries_grad, terms[0], terms[1]], axis=1)
    qkv_part = chip_grad(projected_grad, normed1)
    projected_sum = jnp.sum(projected_grad.astype(F32), axis=0)
    normed1_grad = mat(projected_grad, wqkv)
    gain_one_grad = jnp.sum(normed1_grad * unit1, axis=0)
    shift_one_grad = jnp.sum(normed1_grad, axis=0)
    input_grad = middle_grad + norm_back(normed1_grad, unit1, scale1, gain_one)
    state_grad = (input_grad * state_slope).astype(BF16)
    conv2_part = chip_grad(state_grad, state_taps)
    b2_grad = jnp.sum(state_grad.astype(F32), axis=0)
    taps_grad = mat(state_grad, w2)
    prev_grad = taps_grad[:, :width].reshape(2, states, width)
    odd_grad = taps_grad[:, 2 * width :].reshape(2, states, width)
    odd_grad = odd_grad + jnp.pad(prev_grad[:, 1:], ((0, 0), (0, 1), (0, 0)))
    main_grad = jnp.concatenate(
        [taps_grad[:, width : 2 * width], odd_grad.reshape(rows, width)], axis=0
    )
    main_grad = (main_grad * frame_slope[: 2 * rows]).astype(BF16)
    edge_grad = (prev_grad[:, 0] * edge_slope).astype(BF16)
    edge_grad = jnp.pad(edge_grad, ((0, ROWS - 2), (0, 0)))
    frame_grad = jnp.concatenate([main_grad, edge_grad], axis=0)
    b1_grad = jnp.sum(frame_grad.astype(F32), axis=0)

    blocks = frame_grad.reshape(-1, y_size, 2, share)
    sent, kept = pick(blocks, 1 - core, 2), pick(blocks, core, 2)
    product = lambda g: jnp.einsum("ryn,rk->ynk", g, taps, preferred_element_type=F32)
    got = xor_swap(product(sent).astype(BF16), "tm", 1)
    conv1_part = (product(kept) + got.astype(F32)).astype(BF16).reshape(y_size, -1, width)

    vec_grads = [
        b1_grad,
        b2_grad,
        gain_one_grad,
        shift_one_grad,
        projected_sum[:width],
        projected_sum[2 * width :],
        bout_grad,
        gain_two_grad,
        shift_two_grad,
        bfc2_grad,
        bfc1_grad,
    ]
    vec_part = jnp.concatenate([v.reshape(y_size, 2, -1) for v in vec_grads], axis=2)
    got = xor_swap(pick(vec_part, 1 - core, 1), "tm", 1)
    vec_part = (pick(vec_part, core, 1) + got).astype(BF16)
    vec_part = jnp.pad(vec_part, ((0, 0), (0, -vec_part.shape[1] % width)))
    vec_part = vec_part.reshape(y_size, -1, width)
    qkv_sum, conv2_sum, conv1_sum, vec_sum = all_sum([qkv_part, conv2_part, conv1_part, vec_part])

    taps_back = mat(frame_grad, w1)
    tap = lambda a, i: a[..., i * mels : (i + 1) * mels]
    even_back = taps_back[:rows].reshape(2, states, -1)
    odd_back = taps_back[rows : 2 * rows].reshape(2, states, -1)
    edge_back = taps_back[2 * rows : 2 * rows + 2]
    even_mel = tap(even_back, 1) + tap(odd_back, 0)
    even_mel = even_mel + jnp.concatenate(
        [tap(edge_back, 2)[:, None], tap(odd_back, 2)[:, :-1]], axis=1
    )
    odd_mel = tap(even_back, 2) + tap(odd_back, 1)
    odd_mel = odd_mel + jnp.pad(tap(even_back, 0)[:, 1:], ((0, 0), (0, 1), (0, 0)))
    to_before = jnp.stack([tap(edge_back, 0), tap(even_back, 0)[:, 0] + tap(edge_back, 1)], axis=1)
    to_after = tap(odd_back, 2)[:, -1]
    from_before, from_after = neighbours(to_before, to_after)
    even_mel = even_mel.at[:, 0].add(from_before).at[:, -1].add(from_after[:, 0])
    odd_mel = odd_mel.at[:, -1].add(from_after[:, 1])
    mel_back = jnp.stack([even_mel, odd_mel], axis=2).reshape(2, frames, mels)
    mel_back = jnp.where(frame_valid, mel_back, 0.0).astype(BF16)
    mel_grad = unswapped(mel_back)

    vec_flat = vec_sum.reshape(-1)
    vec_out = [vec_flat[i * share : (i + 1) * share] for i in range(10)]
    vec_out.append(vec_flat[10 * share : 10 * share + fc1_bias.shape[0]])
    conv1_out = conv1_sum.reshape(share, -1)[:, : 3 * mels].T.reshape(3, mels, share)
    conv2_out = conv2_sum.reshape(share, 3 * width).T.reshape(3, width, share)
    return (
        out_states,
        mel_grad,
        conv1_out,
        vec_out[0],
        conv2_out,
        vec_out[1],
        vec_out[2],
        vec_out[3],
        qkv_sum.T,
        vec_out[4],
        vec_out[5],
        out_sum.T,
        vec_out[6],
        vec_out[7],
        vec_out[8],
        fc1_sum.T,
        vec_out[10],
        fc2_sum.reshape(share, hidden).T,
        vec_out[9],
    )


def solution(mesh):
    return jax.shard_map(
        per_device,
        mesh=mesh,
        in_specs=(
            P("clip", "tm", None),
            P("clip"),
            P(None, None, "tm"),
            P("tm"),
            P(None, None, "tm"),
            P("tm"),
            P("tm"),
            P("tm"),
            P(None, "tm"),
            P("tm"),
            P("tm"),
            P(None, "tm"),
            P("tm"),
            P("tm"),
            P("tm"),
            P(None, "tm"),
            P("tm"),
            P(None, "tm"),
            P("tm"),
            P("clip", "tm", None),
        ),
        out_specs=(
            P("clip", "tm", None),
            P("clip", "tm", None),
            P(None, None, "tm"),
            P("tm"),
            P(None, None, "tm"),
            P("tm"),
            P("tm"),
            P("tm"),
            P(None, "tm"),
            P("tm"),
            P("tm"),
            P(None, "tm"),
            P("tm"),
            P("tm"),
            P("tm"),
            P(None, "tm"),
            P("tm"),
            P(None, "tm"),
            P("tm"),
        ),
        check_vma=False,
    )
```

time: 1750 us -> 658 us (0.38)
  blocking collectives: 615 us -> 0 us
  local copies, waits for them, and re-layouts: 565 us -> 152 us
  other arithmetic: 170 us -> 73.5 us
  waiting for transfers between devices: 191 us -> 242 us
  matrix products: 167 us -> 142 us
  starting transfers between devices: 12.3 us -> 33.5 us
    unnamed x2 -> x0, blocking collectives: 601 us -> none
    unnamed x176, local copies, waits for them, and re-layouts: 294 us -> 18.6 us
    ppermute x6 -> x45, waiting for transfers between devices: 3.08 us -> 242 us  [xor_swap(): return lax.ppermute(array, axis, [(i, i ^ mask) for i in range(size)])]
    reshape x31 -> x24, local copies, waits for them, and re-layouts: 210 us -> 24.5 us  [the longest x1 8.28 us: chip_grad(): blocks = grad.reshape(rows, y_size, 2, -1)]
    all_gather x8 -> x0, waiting for transfers between devices: 186 us -> none  [the longest x1 117 us: per_device(): lax.all_gather(summed_share.astype(jnp.bfloat16), 'clip', axis=0, tiled=T...]
    reshape x1 -> x4, other arithmetic: 97.2 us -> 1.03 us  [the longest x1 0.91 us: per_device(): conv1_sum.reshape(share, -1)[:, :3 * mels].T.reshape(3, mels, share)]
    dot_general x24 -> x29, matrix products: 167 us -> 129 us  [the longest x10 38 us: chip_grad(): jnp.einsum('ryn,rk->ynk', g, acts, preferred_element_type=F32)]
    dynamic_update_slice x0 -> x28, local copies, waits for them, and re-layouts: none -> 32.3 us  [the longest x14 18.4 us: gather_rows(): lax.dynamic_update_slice(whole, other[i][None], (place ^ mask ^ 1, 0, 0))]
  transfers between devices with their start and end apart: 16 -> 45, of which waited for: 7 -> 17; matrix products, arithmetic and copies ran while one was open for 17% -> 38% of each run, Pallas kernels for 0% -> 0%
where the time goes in v1:
time: 658 us; the launch traced here: 647 us
  waiting for transfers between devices  242 us (37%)
  local copies, waits for them, and re-layouts  152 us (23%)
  matrix products  142 us (22%)
  other arithmetic  73.5 us (11%)
  starting transfers between devices  33.5 us (5%)
    ppermute x45, waiting for transfers between devices, xor_swap(): return lax.ppermute(array, axis, [(i, i ^ mask) for i in range(size)])  242 us
    dot_general x10, matrix products, chip_grad(): jnp.einsum('ryn,rk->ynk', g, acts, preferred_element_type=F32)  38 us
    ppermute x45, starting transfers between devices, xor_swap(): return lax.ppermute(array, axis, [(i, i ^ mask) for i in range(size)])  33.5 us
    dot_general x6, matrix products, mat_t(): lax.dot_general(a, b, (((1,), (1,)), ((), ())), preferred_element_type=F32)  30 us
    dynamic_slice x9, local copies, waits for them, and re-layouts, pick(): return lax.dynamic_index_in_dim(array, index, axis=axis, keepdims=False)  26.1 us
    dot_general x6, matrix products, mat(): return jnp.dot(a, b, preferred_element_type=F32)  19.9 us
    unnamed x176, local copies, waits for them, and re-layouts  18.6 us
    dynamic_update_slice x14, local copies, waits for them, and re-layouts, gather_rows(): lax.dynamic_update_slice(whole, other[i][None], (place ^ mask ^ 1, 0, 0))  18.4 us
  transfers between devices with their start and end apart: 45, of which 17 were waited for; matrix products, arithmetic and copies ran while one was open for 38% of the time, Pallas kernels for 0%

profile of v1, /device:TPU:0, one launch (start us, length us, event | category | flops | bytes accessed | tf_op | source)
XLA Modules:
  0.0 646.7 jit_solution(9382313173358099420)
XLA Ops:
  0.7 7.5 %concatenate.93 = bf16[2688]{0:T(1024)(128)(2,1)S(1)} concatenate(bf16[192]{0:T(256)(128)(2,1)} %param.29, bf16[192]{0:T(256)(128)(2,1)} %param.31, bf16[192]{0:T(256)(128)(2,1)} %param.32, bf16[192]{0:T(256)(128)(2,1)} %param.33, bf16[192]{0:T(256)(128)(2,1)} %param.35, bf16[192]{0:T(256)(128)(2,1)} %param.36, bf16[192]{0:T(256)(128)(2,1)} %param.38, bf16[192]{0:T(256)(128)(2,1)} %param.39, ...), dimensions={0} | concatenate | bytes 10752 | tf_op jit(solution)/shard_map/concatenate | solution.py:145
  28.3 3.8 multiply_sine_fusion
  50.1 3.1 broadcast_select_fusion.1
  61.5 4.9 concatenate.92
  76.1 5.4 fusion.29
  85.7 11.5 %collective-permute-done.19 = bf16[256,768]{1,0:T(8,128)(2,1)} collective-permute-done((bf16[256,768]{1,0:T(8,128)(2,1)}, bf16[256,768]{1,0:T(8,128)(2,1)}, u32[]{:S(2)}, u32[]{:S(2)}) %collective-permute-start.19) | collective-permute-done | bytes 393248 | tf_op jit(solution)/shard_map/ppermute | solution.py:18
  102.5 3.3 select_n.458
  115.0 8.8 %collective-permute-done.16 = bf16[192,3072]{1,0:T(8,128)(2,1)} collective-permute-done((bf16[192,3072]{1,0:T(8,128)(2,1)S(1)}, bf16[192,3072]{1,0:T(8,128)(2,1)}, u32[]{:S(2)}, u32[]{:S(2)}) %collective-permute-start.16) | collective-permute-done | bytes 1179680 | tf_op jit(solution)/shard_map/ppermute | solution.py:18
  131.0 4.2 fusion.132
  140.0 4.3 fusion.20
  165.9 13.9 %fusion.145 = (f32[12,512]{1,0:T(8,128)S(1)}, f32[12,512,1024]{2,1,0:T(8,128)}) fusion(pred[1024]{0:T(1024)(128)(4,1)S(1)} %copy-done.71, bf16[512,12,64]{0,2,1:T(8,128)(2,1)} %bitcast.442, bf16[1024,12,64]{0,2,1:T(8,128)(2,1)S(1)} %bitcast.422), kind=kOutput, calls=%fused_computation.365 | convolution fusion | flops 830473216 | bytes 27550720 | tf_op jit(solution)/shard_map/sub | solution.py:268
  179.8 9.9 %divide_convert_fusion = bf16[12,512,1024]{2,1,0:T(8,128)(2,1)S(1)} fusion(f32[12,512,1024]{2,1,0:T(8,128)} %get-tuple-element.238, f32[12,512]{1,0:T(8,128)S(1)} %get-tuple-element.237), kind=kLoop, calls=%fused_computation.2 | loop fusion | flops 12582912 | bytes 37773312 | tf_op jit(solution)/shard_map/convert_element_type | solution.py:269
  189.7 7.4 %convolution_convert_fusion.6 = bf16[12,64,512]{2,1,0:T(8,128)(2,1)} fusion(bf16[1024,12,64]{0,2,1:T(8,128)(2,1)} %bitcast.399, bf16[12,512,1024]{2,1,0:T(8,128)(2,1)S(1)} %divide_convert_fusion), kind=kOutput, calls=%fused_computation.126 | convolution fusion | flops 805699584 | bytes 14942208 | tf_op jit(solution)/shard_map/hqk,khd->qhd/dot_general | solution.py:270
  197.2 3.1 fusion.146
  200.6 10.3 %multiply_convert_fusion.2 = (bf16[512,3072]{1,0:T(8,128)(2,1)}, f32[512,3072]{1,0:T(8,128)S(1)}) fusion(f32[3072]{0:T(1024)S(1)} %add.656, bf16[3072,768]{1,0:T(8,128)(2,1)} %bitcast.430, f32[512,768]{1,0:T(8,128)S(1)} %get-tuple-element.240, f32[768]{0:T(1024)S(1)} %copy-done.68, f32[768]{0:T(1024)S(1)} %mul.439, f32[512]{0:T(512)S(1)} %add_rsqrt_fusion, ...), kind=kOutput, calls=%fused_computation.28 | convolution fusion | flops 2454061056 | bytes 15751168 | tf_op jit(solution)/shard_map/dot_general | solution.py:68
  211.0 7.8 %convert_reduce_fusion = (f32[3072]{0:T(1024)S(1)}, bf16[512,3072]{1,0:T(8,128)(2,1)S(1)}) fusion(f32[512,3072]{1,0:T(8,128)S(1)} %get-tuple-element.242, f32[3072]{0:T(1024)S(1)} %add.656, bf16[512,768]{1,0:T(8,128)(2,1)S(1)} %bitcast.419, bf16[768,3072]{1,0:T(8,128)(2,1)S(1)} %bitcast.436), kind=kOutput, calls=%fused_computation.26 | convolution fusion | flops 2463101952 | bytes 14966784 | tf_op jit(solution)/shard_map/dot_general | solution.py:64
  224.8 8.4 %convolution_convert_fusion.4 = bf16[12,64,1024]{2,1,0:T(8,128)(2,1)} fusion(bf16[512,12,64]{0,2,1:T(8,128)(2,1)S(1)} %bitcast.396, bf16[12,512,1024]{2,1,0:T(8,128)(2,1)} %copy-done), kind=kOutput, calls=%fused_computation.90 | convolution fusion | flops 806092800 | bytes 14942208 | tf_op jit(solution)/shard_map/hqk,qhd->khd/dot_general | solution.py:334
  234.6 8.3 %reshape.640 = bf16[512,2,2,768]{3,2,1,0:T(2,128)(2,1)} reshape(bf16[512,3072]{1,0:T(8,128)(2,1)} %copy-done.29) | data formatting | bytes 6291456 | tf_op jit(solution)/shard_map/reshape | solution.py:288
  242.9 7.9 %multiply_convert_fusion = bf16[12,512,1024]{2,1,0:T(8,128)(2,1)S(1)} fusion(bf16[12,512,1024]{2,1,0:T(8,128)(2,1)} %copy-done, f32[12,512]{1,0:T(8,128)S(1)} %bitcast.490, bf16[512,12,64]{0,2,1:T(8,128)(2,1)} %bitcast.398, bf16[1024,12,64]{0,2,1:T(8,128)(2,1)} %bitcast.400), kind=kOutput, calls=%fused_computation.1 | convolution fusion | flops 830472192 | bytes 27549696 | tf_op jit(solution)/shard_map/qhd,khd->hqk/dot_general | solution.py:329
  250.8 4.1 multiply_convert_fusion.4
  260.9 9.1 %constant_dynamic-slice_fusion.3 = (bf16[512,2,1,768]{3,2,1,0:T(2,128)(2,1)}, bf16[512,2,1,768]{3,2,1,0:T(2,128)(2,1)}) fusion(bf16[512,2,2,768]{3,2,1,0:T(2,128)(2,1)S(1)} %copy-done.2, s32[]{:T(128)S(6)} %select_n.441, s32[]{:T(128)S(6)} %select_n.442), kind=kLoop, calls=%fused_computation.244 | loop fusion | bytes 6291464 | tf_op jit(solution)/shard_map/jit(dynamic_index_in_dim)/dynamic_slice | solution.py:22
  269.9 8.5 %copy.168 = bf16[512,2,1,768]{0,3,1,2:T(8,128)(2,1)} copy(bf16[512,2,1,768]{3,2,1,0:T(2,128)(2,1)} %get-tuple-element.141) | data formatting | bytes 3145728 | tf_op jit(solution)/shard_map/jit(dynamic_index_in_dim)/dynamic_slice | solution.py:22
  278.5 5.0 convolution_convert_fusion.2
  283.7 6.1 copy.167
  289.8 4.9 convolution_convert_fusion
  295.1 8.6 %multiply_convert_fusion.5 = bf16[12,64,512]{2,1,0:T(8,128)(2,1)S(1)} fusion(bf16[1024,12,64]{0,2,1:T(8,128)(2,1)S(1)} %bitcast.423, bf16[12,512,1024]{2,1,0:T(8,128)(2,1)} %copy-done.1), kind=kOutput, calls=%fused_computation.113 | convolution fusion | flops 806092800 | bytes 14942208 | tf_op jit(solution)/shard_map/hqk,khd->qhd/dot_general | solution.py:331
  309.9 4.7 multiply_reduce_fusion.1
  329.4 3.7 convolution_convert_fusion.1
  338.6 5.3 add_convert_fusion.1
  343.9 4.5 add_convert_fusion.2
  348.4 5.0 reshape.639
  353.4 3.2 fusion.19
  361.0 3.8 add_convert_fusion.4
  367.5 3.3 add_convert_fusion.5
  380.1 43.1 %collective-permute-done.38 = bf16[1,1792,768]{2,1,0:T(8,128)(2,1)} collective-permute-done((bf16[1,1792,768]{2,1,0:T(8,128)(2,1)}, bf16[1,1792,768]{2,1,0:T(8,128)(2,1)}, u32[]{:S(2)}, u32[]{:S(2)}) %collective-permute-start.38) | collective-permute-done | bytes 2752544 | tf_op jit(solution)/shard_map/ppermute | solution.py:18
  425.8 39.5 %collective-permute-done.28 = bf16[1,1280,768]{2,1,0:T(8,128)(2,1)S(1)} collective-permute-done((bf16[1,1280,768]{2,1,0:T(8,128)(2,1)S(1)}, bf16[1,1280,768]{2,1,0:T(8,128)(2,1)S(1)}, u32[]{:S(2)}, u32[]{:S(2)}) %collective-permute-start.28) | collective-permute-done | bytes 1966112 | tf_op jit(solution)/shard_map/ppermute | solution.py:18
  469.4 21.2 %collective-permute-done.29 = bf16[1,4,160,768]{3,2,1,0:T(8,128)(2,1)S(1)} collective-permute-done((bf16[1,4,160,768]{3,2,1,0:T(8,128)(2,1)S(1)}, bf16[1,4,160,768]{3,2,1,0:T(8,128)(2,1)S(1)}, u32[]{:S(2)}, u32[]{:S(2)}) %collective-permute-start.29) | collective-permute-done | bytes 983072 | tf_op jit(solution)/shard_map/ppermute | solution.py:18
  492.6 25.0 %collective-permute-done.39 = bf16[1,4,224,768]{3,2,1,0:T(8,128)(2,1)S(1)} collective-permute-done((bf16[1,4,224,768]{3,2,1,0:T(8,128)(2,1)S(1)}, bf16[1,4,224,768]{3,2,1,0:T(8,128)(2,1)S(1)}, u32[]{:S(2)}, u32[]{:S(2)}) %collective-permute-start.39) | collective-permute-done | bytes 1376288 | tf_op jit(solution)/shard_map/ppermute | solution.py:18
  522.6 14.9 %collective-permute-done.31 = bf16[1,160,768]{2,1,0:T(8,128)(2,1)S(1)} collective-permute-done((bf16[1,160,768]{2,1,0:T(8,128)(2,1)S(1)}, bf16[1,160,768]{2,1,0:T(8,128)(2,1)S(1)}, u32[]{:S(2)}, u32[]{:S(2)}) %collective-permute-start.31) | collective-permute-done | bytes 245792 | tf_op jit(solution)/shard_map/ppermute | solution.py:18
  537.5 3.5 collective-permute-start.32
  541.4 16.9 %collective-permute-done.32 = bf16[1,160,768]{2,1,0:T(8,128)(2,1)S(1)} collective-permute-done((bf16[1,160,768]{2,1,0:T(8,128)(2,1)S(1)}, bf16[1,160,768]{2,1,0:T(8,128)(2,1)S(1)}, u32[]{:S(2)}, u32[]{:S(2)}) %collective-permute-start.32) | collective-permute-done | bytes 245792 | tf_op jit(solution)/shard_map/ppermute | solution.py:18
  558.5 7.2 %collective-permute-done.41 = bf16[1,224,768]{2,1,0:T(8,128)(2,1)S(1)} collective-permute-done((bf16[1,224,768]{2,1,0:T(8,128)(2,1)S(1)}, bf16[1,224,768]{2,1,0:T(8,128)(2,1)S(1)}, u32[]{:S(2)}, u32[]{:S(2)}) %collective-permute-start.41) | collective-permute-done | bytes 344096 | tf_op jit(solution)/shard_map/ppermute | solution.py:18
  566.5 11.5 %collective-permute-done.33 = bf16[2,160,768]{2,1,0:T(8,128)(2,1)S(1)} collective-permute-done((bf16[2,160,768]{2,1,0:T(8,128)(2,1)S(1)}, bf16[2,160,768]{2,1,0:T(8,128)(2,1)S(1)}, u32[]{:S(2)}, u32[]{:S(2)}) %collective-permute-start.33) | collective-permute-done | bytes 491552 | tf_op jit(solution)/shard_map/ppermute | solution.py:18
  578.1 6.0 collective-permute-done.42
  588.1 3.3 collective-permute-done.23
  592.3 8.5 %collective-permute-done.43 = bf16[2,224,768]{2,1,0:T(8,128)(2,1)S(1)} collective-permute-done((bf16[2,224,768]{2,1,0:T(8,128)(2,1)S(1)}, bf16[2,224,768]{2,1,0:T(8,128)(2,1)S(1)}, u32[]{:S(2)}, u32[]{:S(2)}) %collective-permute-start.43) | collective-permute-done | bytes 688160 | tf_op jit(solution)/shard_map/ppermute | solution.py:18
  602.7 6.6 %collective-permute-done.34 = bf16[1,4,160,768]{3,2,1,0:T(8,128)(2,1)} collective-permute-done((bf16[1,4,160,768]{3,2,1,0:T(8,128)(2,1)S(1)}, bf16[1,4,160,768]{3,2,1,0:T(8,128)(2,1)}, u32[]{:S(2)}, u32[]{:S(2)}) %collective-permute-start.34) | collective-permute-done | bytes 983072 | tf_op jit(solution)/shard_map/ppermute | solution.py:18
  620.0 16.9 %collective-permute-done.44 = bf16[1,4,224,768]{3,2,1,0:T(8,128)(2,1)} collective-permute-done((bf16[1,4,224,768]{3,2,1,0:T(8,128)(2,1)S(1)}, bf16[1,4,224,768]{3,2,1,0:T(8,128)(2,1)}, u32[]{:S(2)}, u32[]{:S(2)}) %collective-permute-start.44) | collective-permute-done | bytes 1376288 | tf_op jit(solution)/shard_map/ppermute | solution.py:18
  (494 shorter events, 205.9 us)
Async XLA Ops:
  8.2 32.9 %collective-permute-start.5 = (bf16[21,128]{1,0:T(8,128)(2,1)S(1)}, bf16[21,128]{1,0:T(8,128)(2,1)S(1)}, u32[]{:S(2)}, u32[]{:S(2)}) collective-permute-start(bf16[21,128]{1,0:T(8,128)(2,1)S(1)} %bitcast.493), channel_id=1, source_target_pairs={{0,2},{1,3},{2,0},{3,1},{4,6},{5,7},{6,4},{7,5},{8,10},{9,11},{10,... | collective-permute-start | bytes 16136 | tf_op jit(solution)/shard_map/ppermute | solution.py:18
  12.4 70.1 %collective-permute-start.7 = (bf16[192,2304]{1,0:T(8,128)(2,1)S(1)}, bf16[192,2304]{1,0:T(8,128)(2,1)}, u32[]{:S(2)}, u32[]{:S(2)}) collective-permute-start(bf16[192,2304]{1,0:T(8,128)(2,1)S(1)} %bitcast.410), channel_id=1, source_target_pairs={{0,2},{1,3},{2,0},{3,1},{4,6},{5,7},{6,4},{7,5},{8,10},{9,11},{10,... | collective-permute-start | bytes 2654216 | tf_op jit(solution)/shard_map/ppermute | solution.py:18
  14.0 44.1 %collective-permute-start.3 = (bf16[192,256]{0,1:T(8,128)(2,1)}, bf16[192,256]{0,1:T(8,128)(2,1)}, u32[]{:S(2)}, u32[]{:S(2)}) collective-permute-start(bf16[192,256]{0,1:T(8,128)(2,1)} %get-tuple-element.194), channel_id=1, source_target_pairs={{0,2},{1,3},{2,0},{3,1},{4,6},{5,7},{6,4},{7,5},{8,10},{9,11},{10,... | collective-permute-start | bytes 294920 | tf_op jit(solution)/shard_map/ppermute | solution.py:18
  16.7 32.2 %collective-permute-start = (bf16[512,80]{0,1:T(8,128)(2,1)}, bf16[512,80]{0,1:T(8,128)(2,1)}, u32[]{:S(2)}, u32[]{:S(2)}) collective-permute-start(bf16[512,80]{0,1:T(8,128)(2,1)} %get-tuple-element.191), channel_id=1, source_target_pairs={{0,2},{1,3},{2,0},{3,1},{4,6},{5,7},{6,4},{7,5},{8,10},{9,11},{10,... | collective-permute-start | bytes 245768 | tf_op jit(solution)/shard_map/ppermute | solution.py:18
  16.7 89.1 %collective-permute-start.9 = (bf16[576,768]{1,0:T(8,128)(2,1)}, bf16[576,768]{1,0:T(8,128)(2,1)}, u32[]{:S(2)}, u32[]{:S(2)}) collective-permute-start(bf16[576,768]{1,0:T(8,128)(2,1)} %bitcast.28), channel_id=1, source_target_pairs={{0,2},{1,3},{2,0},{3,1},{4,6},{5,7},{6,4},{7,5},{8,10},{9,11},{10,... | collective-permute-start | bytes 2654216 | tf_op jit(solution)/shard_map/ppermute | solution.py:18
  41.6 4.0 collective-permute-start.6
  45.6 24.6 %collective-permute-start.12 = (bf16[192,768]{1,0:T(8,128)(2,1)}, bf16[192,768]{1,0:T(8,128)(2,1)}, u32[]{:S(2)}, u32[]{:S(2)}) collective-permute-start(bf16[192,768]{1,0:T(8,128)(2,1)} %bitcast.468), channel_id=1, source_target_pairs={{0,2},{1,3},{2,0},{3,1},{4,6},{5,7},{6,4},{7,5},{8,10},{9,11},{10,... | collective-permute-start | bytes 884744 | tf_op jit(solution)/shard_map/ppermute | solution.py:18
  46.5 84.4 %copy-start.61 = (f32[768]{0:T(1024)}, f32[768]{0:T(1024)S(1)}, u32[]{:S(2)}) copy-start(f32[768]{0:T(1024)S(1)} %add.618) | copy-start | bytes 9220
  53.6 1.4 collective-permute-start.2
  55.0 1.1 collective-permute-start.1
  56.1 54.6 %collective-permute-start.14 = (bf16[768,768]{1,0:T(8,128)(2,1)S(1)}, bf16[768,768]{1,0:T(8,128)(2,1)}, u32[]{:S(2)}, u32[]{:S(2)}) collective-permute-start(bf16[768,768]{1,0:T(8,128)(2,1)S(1)} %bitcast.408), channel_id=1, source_target_pairs={{0,2},{1,3},{2,0},{3,1},{4,6},{5,7},{6,4},{7,5},{8,10},{9,11},{10,... | collective-permute-start | bytes 3538952 | tf_op jit(solution)/shard_map/ppermute | solution.py:18
  59.8 8.2 %collective-permute-start.4 = (bf16[2,192,256]{1,2,0:T(8,128)(2,1)}, bf16[2,192,256]{1,2,0:T(8,128)(2,1)}, u32[]{:S(2)}, u32[]{:S(2)}) collective-permute-start(bf16[2,192,256]{1,2,0:T(8,128)(2,1)} %pad_maximum_fusion.17), channel_id=1, source_target_pairs={{0,1},{1,0},{2,3},{3,2},{4,5},{5,4},{6,7},{7,6},{8,9},{9,8},{10,11... | collective-permute-start | bytes 589832 | tf_op jit(solution)/shard_map/ppermute | solution.py:18
  68.1 29.1 %collective-permute-start.19 = (bf16[256,768]{1,0:T(8,128)(2,1)}, bf16[256,768]{1,0:T(8,128)(2,1)}, u32[]{:S(2)}, u32[]{:S(2)}) collective-permute-start(bf16[256,768]{1,0:T(8,128)(2,1)} %get-tuple-element.168), channel_id=1, source_target_pairs={{0,2},{1,3},{2,0},{3,1},{4,6},{5,7},{6,4},{7,5},{8,10},{9,11},{10,... | collective-permute-start | bytes 1179656 | tf_op jit(solution)/shard_map/ppermute | solution.py:18
  72.1 35.6 %collective-permute-start.13 = (bf16[2,192,768]{2,1,0:T(8,128)(2,1)}, bf16[2,192,768]{2,1,0:T(8,128)(2,1)}, u32[]{:S(2)}, u32[]{:S(2)}) collective-permute-start(bf16[2,192,768]{2,1,0:T(8,128)(2,1)} %pad_maximum_fusion.13), channel_id=1, source_target_pairs={{0,1},{1,0},{2,3},{3,2},{4,5},{5,4},{6,7},{7,6},{8,9},{9,8},{10,11... | collective-permute-start | bytes 1769480 | tf_op jit(solution)/shard_map/ppermute | solution.py:18
  85.3 41.6 %collective-permute-start.8 = (bf16[2,192,2304]{2,1,0:T(8,128)(2,1)}, bf16[2,192,2304]{2,1,0:T(8,128)(2,1)}, u32[]{:S(2)}, u32[]{:S(2)}) collective-permute-start(bf16[2,192,2304]{2,1,0:T(8,128)(2,1)} %pad_maximum_fusion.6), channel_id=1, source_target_pairs={{0,1},{1,0},{2,3},{3,2},{4,5},{5,4},{6,7},{7,6},{8,9},{9,8},{10,11... | collective-permute-start | bytes 5308424 | tf_op jit(solution)/shard_map/ppermute | solution.py:18
  97.2 26.6 %collective-permute-start.16 = (bf16[192,3072]{1,0:T(8,128)(2,1)S(1)}, bf16[192,3072]{1,0:T(8,128)(2,1)}, u32[]{:S(2)}, u32[]{:S(2)}) collective-permute-start(bf16[192,3072]{1,0:T(8,128)(2,1)S(1)} %bitcast.440), channel_id=1, source_target_pairs={{0,2},{1,3},{2,0},{3,1},{4,6},{5,7},{6,4},{7,5},{8,10},{9,11},{10,... | collective-permute-start | bytes 3538952 | tf_op jit(solution)/shard_map/ppermute | solution.py:18
  107.6 27.9 %collective-permute-start.10 = (bf16[2,576,768]{2,1,0:T(8,128)(2,1)S(1)}, bf16[2,576,768]{2,1,0:T(8,128)(2,1)S(1)}, u32[]{:S(2)}, u32[]{:S(2)}) collective-permute-start(bf16[2,576,768]{2,1,0:T(8,128)(2,1)S(1)} %pad_maximum_fusion.7), channel_id=1, source_target_pairs={{0,1},{1,0},{2,3},{3,2},{4,5},{5,4},{6,7},{7,6},{8,9},{9,8},{10,11... | collective-permute-start | bytes 5308424 | tf_op jit(solution)/shard_map/ppermute | solution.py:18
  114.5 32.8 %collective-permute-start.15 = (bf16[2,768,768]{2,1,0:T(8,128)(2,1)}, bf16[2,768,768]{2,1,0:T(8,128)(2,1)}, u32[]{:S(2)}, u32[]{:S(2)}) collective-permute-start(bf16[2,768,768]{2,1,0:T(8,128)(2,1)} %pad_maximum_fusion.2), channel_id=1, source_target_pairs={{0,1},{1,0},{2,3},{3,2},{4,5},{5,4},{6,7},{7,6},{8,9},{9,8},{10,11... | collective-permute-start | bytes 7077896 | tf_op jit(solution)/shard_map/ppermute | solution.py:18
  126.9 25.2 %collective-permute-start.17 = (bf16[2,192,3072]{2,1,0:T(8,128)(2,1)}, bf16[2,192,3072]{2,1,0:T(8,128)(2,1)}, u32[]{:S(2)}, u32[]{:S(2)}) collective-permute-start(bf16[2,192,3072]{2,1,0:T(8,128)(2,1)} %pad_maximum_fusion.3), channel_id=1, source_target_pairs={{0,1},{1,0},{2,3},{3,2},{4,5},{5,4},{6,7},{7,6},{8,9},{9,8},{10,11... | collective-permute-start | bytes 7077896 | tf_op jit(solution)/shard_map/ppermute | solution.py:18
  145.8 15.8 %collective-permute-start.11 = (bf16[2,512,768]{2,1,0:T(8,128)(2,1)}, bf16[2,512,768]{2,1,0:T(8,128)(2,1)}, u32[]{:S(2)}, u32[]{:S(2)}) collective-permute-start(bf16[2,512,768]{2,1,0:T(8,128)(2,1)} %pad_maximum_fusion.9), channel_id=1, source_target_pairs={{0,1},{1,0},{2,3},{3,2},{4,5},{5,4},{6,7},{7,6},{8,9},{9,8},{10,11... | collective-permute-start | bytes 4718600 | tf_op jit(solution)/shard_map/ppermute | solution.py:18
  257.5 48.7 %collective-permute-start.20 = (bf16[2,512,768]{1,2,0:T(8,128)(2,1)}, bf16[2,512,768]{1,2,0:T(8,128)(2,1)}, u32[]{:S(2)}, u32[]{:S(2)}) collective-permute-start(bf16[2,512,768]{1,2,0:T(8,128)(2,1)} %pad_maximum_fusion.8), channel_id=1, source_target_pairs={{0,1},{1,0},{2,3},{3,2},{4,5},{5,4},{6,7},{7,6},{8,9},{9,8},{10,11... | collective-permute-start | bytes 4718600 | tf_op jit(solution)/shard_map/ppermute | solution.py:18
  260.5 43.2 %collective-permute-start.37 = (bf16[2,192,768]{2,1,0:T(8,128)(2,1)}, bf16[2,192,768]{2,1,0:T(8,128)(2,1)}, u32[]{:S(2)}, u32[]{:S(2)}) collective-permute-start(bf16[2,192,768]{2,1,0:T(8,128)(2,1)} %convolution_convert_fusion.7), channel_id=1, source_target_pairs={{0,1},{1,0},{2,3},{3,2},{4,5},{5,4},{6,7},{7,6},{8,9},{9,8},{10,11... | collective-permute-start | bytes 1769480 | tf_op jit(solution)/shard_map/ppermute | solution.py:18
  283.5 55.1 %collective-permute-start.36 = (bf16[2,768,768]{2,1,0:T(8,128)(2,1)}, bf16[2,768,768]{2,1,0:T(8,128)(2,1)}, u32[]{:S(2)}, u32[]{:S(2)}) collective-permute-start(bf16[2,768,768]{2,1,0:T(8,128)(2,1)} %convolution_convert_fusion.2), channel_id=1, source_target_pairs={{0,1},{1,0},{2,3},{3,2},{4,5},{5,4},{6,7},{7,6},{8,9},{9,8},{10,11... | collective-permute-start | bytes 7077896 | tf_op jit(solution)/shard_map/ppermute | solution.py:18
  294.7 49.2 %collective-permute-start.35 = (bf16[2,192,3072]{2,1,0:T(8,128)(2,1)}, bf16[2,192,3072]{2,1,0:T(8,128)(2,1)}, u32[]{:S(2)}, u32[]{:S(2)}) collective-permute-start(bf16[2,192,3072]{2,1,0:T(8,128)(2,1)} %convolution_convert_fusion), channel_id=1, source_target_pairs={{0,1},{1,0},{2,3},{3,2},{4,5},{5,4},{6,7},{7,6},{8,9},{9,8},{10,11... | collective-permute-start | bytes 7077896 | tf_op jit(solution)/shard_map/ppermute | solution.py:18
  324.2 11.4 %collective-permute-start.27 = (f32[2,2688]{1,0:T(2,128)S(1)}, f32[2,2688]{1,0:T(2,128)S(1)}, u32[]{:S(2)}, u32[]{:S(2)}) collective-permute-start(f32[2,2688]{1,0:T(2,128)S(1)} %bitcast.496), channel_id=1, source_target_pairs={{0,1},{1,0},{2,3},{3,2},{4,5},{5,4},{6,7},{7,6},{8,9},{9,8},{10,11... | collective-permute-start | bytes 64520 | tf_op jit(solution)/shard_map/ppermute | solution.py:18
  329.0 7.0 %collective-permute-start.26 = (bf16[2,192,256]{2,1,0:T(8,128)(2,1)}, bf16[2,192,256]{2,1,0:T(8,128)(2,1)}, u32[]{:S(2)}, u32[]{:S(2)}) collective-permute-start(bf16[2,192,256]{2,1,0:T(8,128)(2,1)} %convolution_convert_fusion.8), channel_id=1, source_target_pairs={{0,1},{1,0},{2,3},{3,2},{4,5},{5,4},{6,7},{7,6},{8,9},{9,8},{10,11... | collective-permute-start | bytes 589832 | tf_op jit(solution)/shard_map/ppermute | solution.py:18
  333.1 27.9 %collective-permute-start.25 = (bf16[2,192,2304]{2,1,0:T(8,128)(2,1)}, bf16[2,192,2304]{2,1,0:T(8,128)(2,1)}, u32[]{:S(2)}, u32[]{:S(2)}) collective-permute-start(bf16[2,192,2304]{2,1,0:T(8,128)(2,1)} %convolution_convert_fusion.1), channel_id=1, source_target_pairs={{0,1},{1,0},{2,3},{3,2},{4,5},{5,4},{6,7},{7,6},{8,9},{9,8},{10,11... | collective-permute-start | bytes 5308424 | tf_op jit(solution)/shard_map/ppermute | solution.py:18
  335.6 31.9 %collective-permute-start.24 = (bf16[2,576,768]{2,1,0:T(8,128)(2,1)}, bf16[2,576,768]{2,1,0:T(8,128)(2,1)}, u32[]{:S(2)}, u32[]{:S(2)}) collective-permute-start(bf16[2,576,768]{2,1,0:T(8,128)(2,1)} %convolution_convert_fusion.3), channel_id=1, source_target_pairs={{0,1},{1,0},{2,3},{3,2},{4,5},{5,4},{6,7},{7,6},{8,9},{9,8},{10,11... | collective-permute-start | bytes 5308424 | tf_op jit(solution)/shard_map/ppermute | solution.py:18
  360.4 62.8 %collective-permute-start.38 = (bf16[1,1792,768]{2,1,0:T(8,128)(2,1)}, bf16[1,1792,768]{2,1,0:T(8,128)(2,1)}, u32[]{:S(2)}, u32[]{:S(2)}) collective-permute-start(bf16[1,1792,768]{2,1,0:T(8,128)(2,1)} %constant_dynamic-slice_fusion.1), channel_id=1, source_target_pairs={{0,2},{1,3},{2,0},{3,1},{4,6},{5,7},{6,4},{7,5},{8,10},{9,11},{10,... | collective-permute-start | bytes 8257544 | tf_op jit(solution)/shard_map/ppermute | solution.py:18
  371.4 51.8 %slice-start = ((s8[5505024]{0:T(1024)(128)(4,1)}), s8[4194304]{0:T(1024)(128)(4,1)S(1)}, s32[]{:S(2)}) async-start(s8[5505024]{0:T(1024)(128)(4,1)} %bitcast.390), calls=%async_computation | async-start | bytes 8388608
  371.6 51.6 %slice-start.1 = ((s8[5505024]{0:T(1024)(128)(4,1)}), s8[1310720]{0:T(1024)(128)(4,1)S(1)}, s32[]{:S(2)}) async-start(s8[5505024]{0:T(1024)(128)(4,1)} %bitcast.390), calls=%async_computation.1 | async-start | bytes 2621440
  371.6 93.7 %collective-permute-start.28 = (bf16[1,1280,768]{2,1,0:T(8,128)(2,1)S(1)}, bf16[1,1280,768]{2,1,0:T(8,128)(2,1)S(1)}, u32[]{:S(2)}, u32[]{:S(2)}) collective-permute-start(bf16[1,1280,768]{2,1,0:T(8,128)(2,1)S(1)} %constant_dynamic-slice_fusion.5), channel_id=1, source_target_pairs={{0,2},{1,3},{2,0},{3,1},{4,6},{5,7},{6,4},{7,5},{8,10},{9,11},{10,... | collective-permute-start | bytes 5898248 | tf_op jit(solution)/shard_map/ppermute | solution.py:18
  376.2 210.9 %collective-permute-start.18 = (bf16[256,768]{1,0:T(8,128)(2,1)S(1)}, bf16[256,768]{1,0:T(8,128)(2,1)S(1)}, u32[]{:S(2)}, u32[]{:S(2)}) collective-permute-start(bf16[256,768]{1,0:T(8,128)(2,1)S(1)} %get-tuple-element.171), channel_id=1, source_target_pairs={{0,2},{1,3},{2,0},{3,1},{4,6},{5,7},{6,4},{7,5},{8,10},{9,11},{10,... | collective-permute-start | bytes 1179656 | tf_op jit(solution)/shard_map/ppermute | solution.py:18
  379.8 112.8 %collective-permute-start.21 = (f32[2,80]{1,0:T(2,128)S(1)}, f32[2,80]{1,0:T(2,128)S(1)}, u32[]{:S(2)}, u32[]{:S(2)}) collective-permute-start(f32[2,80]{1,0:T(2,128)S(1)} %bitcast.500), channel_id=1, source_target_pairs={{0,1},{1,0},{2,3},{3,2},{4,5},{5,4},{6,7},{7,6},{8,9},{9,8},{10,11... | collective-permute-start | bytes 1928 | tf_op jit(solution)/shard_map/ppermute | solution.py:18
  465.9 24.8 %collective-permute-start.29 = (bf16[1,4,160,768]{3,2,1,0:T(8,128)(2,1)S(1)}, bf16[1,4,160,768]{3,2,1,0:T(8,128)(2,1)S(1)}, u32[]{:S(2)}, u32[]{:S(2)}) collective-permute-start(bf16[1,4,160,768]{3,2,1,0:T(8,128)(2,1)S(1)} %dynamic-slice_bitcast_fusion.1), channel_id=1, source_target_pairs={{0,4},{4,0},{8,12},{12,8},{16,20},{20,16},{24,28},{28,24},{1,5},{5... | collective-permute-start | bytes 2949128 | tf_op jit(solution)/shard_map/ppermute | solution.py:18
  467.5 50.1 %collective-permute-start.39 = (bf16[1,4,224,768]{3,2,1,0:T(8,128)(2,1)S(1)}, bf16[1,4,224,768]{3,2,1,0:T(8,128)(2,1)S(1)}, u32[]{:S(2)}, u32[]{:S(2)}) collective-permute-start(bf16[1,4,224,768]{3,2,1,0:T(8,128)(2,1)S(1)} %dynamic-slice_bitcast_fusion), channel_id=1, source_target_pairs={{0,4},{4,0},{8,12},{12,8},{16,20},{20,16},{24,28},{28,24},{1,5},{5... | collective-permute-start | bytes 4128776 | tf_op jit(solution)/shard_map/ppermute | solution.py:18
  468.1 54.4 %collective-permute-start.22 = (f32[2,2,80]{2,0,1:T(2,128)S(1)}, f32[2,2,80]{2,0,1:T(2,128)S(1)}, u32[]{:S(2)}, u32[]{:S(2)}) collective-permute-start(f32[2,2,80]{2,0,1:T(2,128)S(1)} %pad_maximum_fusion.22), channel_id=1, source_target_pairs={{0,1},{1,0},{2,3},{3,2},{4,5},{5,4},{6,7},{7,6},{8,9},{9,8},{10,11... | collective-permute-start | bytes 3848 | tf_op jit(solution)/shard_map/ppermute | solution.py:18
  491.0 28.7 %collective-permute-start.30 = (bf16[2,160,768]{2,1,0:T(8,128)(2,1)S(1)}, bf16[2,160,768]{2,1,0:T(8,128)(2,1)S(1)}, u32[]{:S(2)}, u32[]{:S(2)}) collective-permute-start(bf16[2,160,768]{2,1,0:T(8,128)(2,1)S(1)} %dynamic-slice_bitcast_fusion.3), channel_id=1, source_target_pairs={{0,8},{4,12},{8,0},{12,4},{16,24},{20,28},{24,16},{28,20},{1,9},{5... | collective-permute-start | bytes 1474568 | tf_op jit(solution)/shard_map/ppermute | solution.py:18
  518.0 23.0 %collective-permute-start.40 = (bf16[2,224,768]{2,1,0:T(8,128)(2,1)S(1)}, bf16[2,224,768]{2,1,0:T(8,128)(2,1)S(1)}, u32[]{:S(2)}, u32[]{:S(2)}) collective-permute-start(bf16[2,224,768]{2,1,0:T(8,128)(2,1)S(1)} %dynamic-slice_bitcast_fusion.2), channel_id=1, source_target_pairs={{0,8},{4,12},{8,0},{12,4},{16,24},{20,28},{24,16},{28,20},{1,9},{5... | collective-permute-start | bytes 2064392 | tf_op jit(solution)/shard_map/ppermute | solution.py:18
  519.9 17.5 %collective-permute-start.31 = (bf16[1,160,768]{2,1,0:T(8,128)(2,1)S(1)}, bf16[1,160,768]{2,1,0:T(8,128)(2,1)S(1)}, u32[]{:S(2)}, u32[]{:S(2)}) collective-permute-start(bf16[1,160,768]{2,1,0:T(8,128)(2,1)S(1)} %constant_dynamic-slice_fusion.4), channel_id=1, source_target_pairs={{0,16},{4,20},{8,24},{12,28},{16,0},{20,4},{24,8},{28,12},{1,17},{... | collective-permute-start | bytes 737288 | tf_op jit(solution)/shard_map/ppermute | solution.py:18
  537.5 20.8 %collective-permute-start.32 = (bf16[1,160,768]{2,1,0:T(8,128)(2,1)S(1)}, bf16[1,160,768]{2,1,0:T(8,128)(2,1)S(1)}, u32[]{:S(2)}, u32[]{:S(2)}) collective-permute-start(bf16[1,160,768]{2,1,0:T(8,128)(2,1)S(1)} %add_convert_fusion.12), channel_id=1, source_target_pairs={{0,16},{4,20},{8,24},{12,28},{16,0},{20,4},{24,8},{28,12},{1,17},{... | collective-permute-start | bytes 737288 | tf_op jit(solution)/shard_map/ppermute | solution.py:18
  541.3 24.4 %collective-permute-start.41 = (bf16[1,224,768]{2,1,0:T(8,128)(2,1)S(1)}, bf16[1,224,768]{2,1,0:T(8,128)(2,1)S(1)}, u32[]{:S(2)}, u32[]{:S(2)}) collective-permute-start(bf16[1,224,768]{2,1,0:T(8,128)(2,1)S(1)} %constant_dynamic-slice_fusion), channel_id=1, source_target_pairs={{0,16},{4,20},{8,24},{12,28},{16,0},{20,4},{24,8},{28,12},{1,17},{... | collective-permute-start | bytes 1032200 | tf_op jit(solution)/shard_map/ppermute | solution.py:18
  558.4 19.7 %collective-permute-start.33 = (bf16[2,160,768]{2,1,0:T(8,128)(2,1)S(1)}, bf16[2,160,768]{2,1,0:T(8,128)(2,1)S(1)}, u32[]{:S(2)}, u32[]{:S(2)}) collective-permute-start(bf16[2,160,768]{2,1,0:T(8,128)(2,1)S(1)} %maximum_bitcast_fusion.2), channel_id=1, source_target_pairs={{0,8},{4,12},{8,0},{12,4},{16,24},{20,28},{24,16},{28,20},{1,9},{5... | collective-permute-start | bytes 1474568 | tf_op jit(solution)/shard_map/ppermute | solution.py:18
  565.8 18.3 %collective-permute-start.42 = (bf16[1,224,768]{2,1,0:T(8,128)(2,1)S(1)}, bf16[1,224,768]{2,1,0:T(8,128)(2,1)S(1)}, u32[]{:S(2)}, u32[]{:S(2)}) collective-permute-start(bf16[1,224,768]{2,1,0:T(8,128)(2,1)S(1)} %add_convert_fusion.11), channel_id=1, source_target_pairs={{0,16},{4,20},{8,24},{12,28},{16,0},{20,4},{24,8},{28,12},{1,17},{... | collective-permute-start | bytes 1032200 | tf_op jit(solution)/shard_map/ppermute | solution.py:18
  584.2 16.5 %collective-permute-start.43 = (bf16[2,224,768]{2,1,0:T(8,128)(2,1)S(1)}, bf16[2,224,768]{2,1,0:T(8,128)(2,1)S(1)}, u32[]{:S(2)}, u32[]{:S(2)}) collective-permute-start(bf16[2,224,768]{2,1,0:T(8,128)(2,1)S(1)} %maximum_bitcast_fusion.1), channel_id=1, source_target_pairs={{0,8},{4,12},{8,0},{12,4},{16,24},{20,28},{24,16},{28,20},{1,9},{5... | collective-permute-start | bytes 2064392 | tf_op jit(solution)/shard_map/ppermute | solution.py:18
  584.5 24.9 %collective-permute-start.34 = (bf16[1,4,160,768]{3,2,1,0:T(8,128)(2,1)S(1)}, bf16[1,4,160,768]{3,2,1,0:T(8,128)(2,1)}, u32[]{:S(2)}, u32[]{:S(2)}) collective-permute-start(bf16[1,4,160,768]{3,2,1,0:T(8,128)(2,1)S(1)} %bitcast.446), channel_id=1, source_target_pairs={{0,4},{4,0},{8,12},{12,8},{16,20},{20,16},{24,28},{28,24},{1,5},{5... | collective-permute-start | bytes 2949128 | tf_op jit(solution)/shard_map/ppermute | solution.py:18
  586.3 5.0 collective-permute-start.23
  601.1 35.8 %collective-permute-start.44 = (bf16[1,4,224,768]{3,2,1,0:T(8,128)(2,1)S(1)}, bf16[1,4,224,768]{3,2,1,0:T(8,128)(2,1)}, u32[]{:S(2)}, u32[]{:S(2)}) collective-permute-start(bf16[1,4,224,768]{3,2,1,0:T(8,128)(2,1)S(1)} %bitcast.426), channel_id=1, source_target_pairs={{0,4},{4,0},{8,12},{12,8},{16,20},{20,16},{24,28},{28,24},{1,5},{5... | collective-permute-start | bytes 4128776 | tf_op jit(solution)/shard_map/ppermute | solution.py:18
  (80 other events, 448.7 us)

commit v2 on v1

v2 whole, which is shorter than its diff:
```python
import functools
import math

import jax
import jax.numpy as jnp
import numpy as np
from jax import lax
from jax.experimental import pallas as pl
from jax.experimental.pallas import tpu as pltpu
from jax.sharding import PartitionSpec as P

HEADS = 12
HEAD_DIM = 64
F32 = jnp.float32
BF16 = jnp.bfloat16
SCALE = 1.0 / math.sqrt(HEAD_DIM)
TILE = 16
LANES = 128
MESH = pl.DeviceIdType.MESH
ANY = pl.BlockSpec(memory_space=pl.ANY)
VMEM = pl.BlockSpec(memory_space=pltpu.VMEM)


def xor_swap(array, axis, mask):
    size = lax.axis_size(axis)
    return lax.ppermute(array, axis, [(i, i ^ mask) for i in range(size)])


def pick(array, index, axis=0):
    return lax.dynamic_index_in_dim(array, index, axis=axis, keepdims=False)


def bits_of(size):
    return [1 << b for b in range(size.bit_length() - 1)]


def combos(masks):
    found = [0]
    for mask in masks:
        found = found + [m ^ mask for m in found]
    return found


def flip(index, mask):
    return index + mask * (1 - 2 * ((index // mask) % 2))


def flip_all(index, mask):
    for bit in bits_of(2 * mask) if mask else []:
        if mask & bit:
            index = flip(index, bit)
    return index


def gelu_pair(v):
    a = jnp.abs(v) * (1.0 / math.sqrt(2.0))
    t = 1.0 / (1.0 + 0.3275911 * a)
    poly = t * (
        0.254829592
        + t * (-0.284496736 + t * (1.421413741 + t * (-1.453152027 + t * 1.061405429)))
    )
    bell = jnp.exp(-0.5 * v * v)
    tail = 0.5 * poly * bell
    cdf = jnp.where(v >= 0, 1.0 - tail, tail)
    return v * cdf, cdf + v * bell * (1.0 / math.sqrt(2.0 * math.pi))


def norm_parts(v):
    center = v - jnp.mean(v, axis=-1, keepdims=True)
    spread = jnp.mean(center * center, axis=-1, keepdims=True)
    scale = lax.rsqrt(spread + 1e-05)
    return center * scale, scale


def norm_back(grad, unit, scale, gain):
    a = grad * gain
    mean_a = jnp.mean(a, axis=-1, keepdims=True)
    mean_an = jnp.mean(a * unit, axis=-1, keepdims=True)
    return (a - mean_a - unit * mean_an) * scale


def positions(count, width):
    half = width // 2
    rates = np.exp(-(math.log(10000.0) / (half - 1)) * np.arange(half))
    angles = np.arange(count)[:, None] * rates[None, :]
    return np.concatenate([np.sin(angles), np.cos(angles)], axis=1).astype(np.float32)


def mat(a, b):
    return jnp.dot(a, b, preferred_element_type=F32)


def mat_t(a, b):
    return lax.dot_general(a, b, (((1,), (1,)), ((), ())), preferred_element_type=F32)


def mat_l(a, b):
    return lax.dot_general(a, b, (((0,), (0,)), ((), ())), preferred_element_type=F32)


def aligned(index, step):
    return pl.multiple_of(index * step, step)


class Place:
    def __init__(self):
        self.parts = lax.axis_size("tm")
        self.clips = lax.axis_size("clip")
        self.tm = lax.axis_index("tm")
        self.cl = lax.axis_index("clip")
        self.y_size = self.parts // 2
        self.x_size = self.y_size
        self.z_size = self.clips // self.x_size
        self.core = self.tm % 2
        self.y = self.tm // 2
        self.x = self.cl % self.x_size
        self.z = self.cl // self.x_size

    def tm_partner(self, mask):
        return {"tm": flip(self.tm, mask)}

    def clip_partner(self, mask):
        return {"clip": flip(self.cl, mask)}


def greet(partners):
    barrier = pltpu.get_barrier_semaphore()
    for partner in partners:
        pl.semaphore_signal(barrier, inc=1, device_id=partner, device_id_type=MESH)
    pl.semaphore_wait(barrier, len(partners))


class Gather:
    def __init__(self, at, own, full, first, count, sends, receives, base):
        self.at, self.own, self.full = at, own, full
        self.first, self.count = first, count
        self.shard = own.shape[0]
        self.split = at.x_size if count % (TILE * at.x_size) == 0 else 1
        self.sends, self.receives, self.base = sends, receives, base
        self.used = 0
        self.y_masks = [2 * b for b in bits_of(at.y_size)]
        self.x_masks = bits_of(at.x_size) if self.split > 1 else []
        self.y_copies, self.x_copies, self.core_copies = [], [], []
        self.started = []

    @staticmethod
    def slots(parts, split):
        y_size = parts // 2
        ys = y_size - 1
        xs = ys * (split - 1)
        return ys + xs + 1 + ys * split

    def region(self, mask, part):
        rows = self.count // self.split
        index = flip_all(self.at.tm, mask) * self.shard + self.first
        if part is not None:
            index = index + part * rows
        else:
            rows = self.count
        return pl.ds(pl.multiple_of(index, TILE), rows)

    def send(self, source, region, partner):
        slot = self.base + self.used
        self.used += 1
        copy = pltpu.make_async_remote_copy(
            src_ref=source,
            dst_ref=self.full.at[region],
            send_sem=self.sends.at[slot],
            recv_sem=self.receives.at[slot],
            device_id=partner,
            device_id_type=MESH,
        )
        copy.start()
        self.started.append(copy)
        return copy

    def part(self, mask):
        return flip_all(self.at.x, mask) if self.split > 1 else 0

    def start(self):
        at = self.at
        rows = self.count // self.split
        first = pl.multiple_of(self.first + self.part(0) * rows, TILE)
        self.pending = []
        mask = self.y_masks[0]
        copy = self.send(
            self.own.at[pl.ds(first, rows)], self.region(0, self.part(0)), at.tm_partner(mask)
        )
        self.pending.append((copy, mask))
        whole = self.own.at[pl.ds(self.first, self.count)]
        self.core_copies.append(self.send(whole, self.region(0, None), at.tm_partner(1)))

    def relay(self, mask, part):
        region = self.region(mask, part)
        self.core_copies.append(self.send(self.full.at[region], region, self.at.tm_partner(1)))

    def after_y(self):
        at = self.at
        have = []
        for i, mask in enumerate(self.y_masks):
            for copy, m in self.pending:
                copy.wait_recv()
                have.append(m)
            self.pending = []
            if i + 1 < len(self.y_masks):
                after = self.y_masks[i + 1]
                for m in [0] + have:
                    region = self.region(m, self.part(0))
                    if m == 0:
                        rows = self.count // self.split
                        first = pl.multiple_of(self.first + self.part(0) * rows, TILE)
                        source = self.own.at[pl.ds(first, rows)]
                    else:
                        source = self.full.at[region]
                    copy = self.send(source, region, at.tm_partner(after))
                    self.pending.append((copy, m ^ after))
        self.have = have
        for x_mask in self.x_masks[:1]:
            for m in have:
                region = self.region(m, self.part(0))
                copy = self.send(self.full.at[region], region, at.clip_partner(x_mask))
                self.x_copies.append((copy, m, x_mask))
        for m in have:
            self.relay(m, self.part(0))

    def after_x(self):
        at = self.at
        got = [0]
        for i, x_mask in enumerate(self.x_masks):
            fresh = []
            for copy, m, q in self.x_copies:
                copy.wait_recv()
                self.relay(m, self.part(q))
                if q not in fresh:
                    fresh.append(q)
            got = got + fresh
            self.x_copies = []
            if i + 1 < len(self.x_masks):
                after = self.x_masks[i + 1]
                for m in self.have:
                    for q in got:
                        region = self.region(m, self.part(q))
                        copy = self.send(self.full.at[region], region, at.clip_partner(after))
                        self.x_copies.append((copy, m, q ^ after))

    def finish(self):
        for copy in self.core_copies:
            copy.wait_recv()

    def close(self):
        for copy in self.started:
            copy.wait_send()


def front_kernel(states, mel_in, w1_own, vec_own, w2_own, wqkv_own, pos_in, *refs):
    (
        w1, vec_raw, vecs, w2, wqkv, taps, x_even, x_odd, slope_even, slope_odd,
        slope_state, block_input, normed, queries, keys, values,
        mel, odd_act, tmp, pos, sends, receives, kv_send, kv_recv, local,
    ) = refs
    at = Place()
    width = block_input.shape[1]
    rows = 2 * states
    block = 256
    mine = at.y % 2
    partners = [at.tm_partner(m) for m in bits_of(at.parts)]
    partners += [at.clip_partner(m) for m in bits_of(at.x_size)]
    seg = [4 * (at.tm // 4) + 2 * s + at.core for s in range(2)]

    locals_ = [
        pltpu.make_async_copy(mel_in.at[mine], mel.at[mine], local.at[0]),
        pltpu.make_async_copy(w1_own, w1.at[pl.ds(aligned(at.tm, w1_own.shape[0]), w1_own.shape[0])], local.at[1]),
        pltpu.make_async_copy(vec_own, vec_raw.at[pl.ds(aligned(at.tm, TILE), TILE)], local.at[2]),
        pltpu.make_async_copy(w2_own, w2.at[pl.ds(aligned(at.tm, w2_own.shape[0]), w2_own.shape[0])], local.at[3]),
        pltpu.make_async_copy(wqkv_own, wqkv.at[pl.ds(aligned(at.tm, wqkv_own.shape[0]), wqkv_own.shape[0])], local.at[4]),
    ]
    for s in range(2):
        locals_.append(
            pltpu.make_async_copy(
                pos_in.at[pl.ds(aligned(seg[s], states), states)],
                pos.at[pl.ds(s * states, states)],
                local.at[5 + s],
            )
        )
    for copy in locals_:
        copy.start()
    greet(partners)
    swap = pltpu.make_async_remote_copy(
        src_ref=mel_in.at[1 - mine],
        dst_ref=mel.at[mine],
        send_sem=kv_send.at[0],
        recv_sem=kv_recv.at[0],
        device_id=at.tm_partner(2),
        device_id_type=MESH,
    )
    swap.start()
    base = 0
    groups = []
    for own, full, pieces in ((w1_own, w1, 1), (vec_own, vec_raw, 1), (w2_own, w2, 2), (wqkv_own, wqkv, 2)):
        count = own.shape[0] // pieces if own.shape[0] % (pieces * TILE * at.x_size) == 0 else own.shape[0]
        for first in range(0, own.shape[0], count):
            g = Gather(at, own, full, first, count, sends, receives, base)
            base += Gather.slots(at.parts, g.split)
            groups.append(g)
    small, large = groups[:2], groups[2:]
    second = [g for g in large if g.own is w2_own]
    third = [g for g in large if g.own is wqkv_own]
    for g in small + second:
        g.start()
    swap.wait_recv()
    locals_[0].wait()
    for s in range(2):
        m = mel[s].astype(F32)
        size = m.shape[0]
        before = pltpu.roll(m, 1, 0)
        after = pltpu.roll(m, size - 1, 0)
        low, high = pl.ds(0, LANES), pl.ds(LANES, LANES)
        even_rows = pl.ds(s * states, states)
        odd_rows = pl.ds(s * size, size)
        x_even[even_rows, low] = before[:states, LANES:].astype(BF16)
        x_even[even_rows, pl.ds(LANES, 2 * LANES)] = m[:states].astype(BF16)
        x_odd[odd_rows, pl.ds(0, 2 * LANES)] = m.astype(BF16)
        x_odd[odd_rows, pl.ds(2 * LANES, LANES)] = after[:, :LANES].astype(BF16)
    for g in small:
        g.after_y()
    for g in second:
        g.after_y()
    for g in third:
        g.start()
    for g in small:
        g.after_x()
        g.finish()
    locals_[1].wait()
    locals_[2].wait()
    total = jnp.zeros(vecs.shape, F32)
    share = width // at.parts
    for j in range(at.parts):
        piece = vec_raw[pl.ds(j * TILE, TILE)].astype(F32)
        low = (j * share) // LANES * LANES
        cells = [piece]
        if low > 0:
            cells = [jnp.zeros((TILE, low), F32)] + cells
        if width - low - piece.shape[1] > 0:
            cells = cells + [jnp.zeros((TILE, width - low - piece.shape[1]), F32)]
        placed = jnp.concatenate(cells, axis=1)
        shift = j * share - low
        total = total + (pltpu.roll(placed, shift, 1) if shift else placed)
    vecs[...] = total

    def vec(i, cols):
        return vecs[pl.ds(i, 1), cols]

    size = states + TILE
    for s in range(2):

        def odd_columns(j, carry, s=s):
            cols = pl.ds(aligned(j, block), block)
            tmp[pl.ds(0, size)] = mat_t(x_odd[pl.ds(s * size, size)], w1[cols])

            def odd_rows(i, carry):
                r = pl.ds(aligned(i, 64), 64)
                act, slope = gelu_pair(tmp[r] + vec(0, cols))
                odd_act[r, cols] = act
                taps[pl.ds(aligned(i, 64) + s * states, 64), pl.ds(2 * width + aligned(j, block), block)] = act.astype(BF16)
                slope_odd[pl.ds(aligned(i, 64) + s * size, 64), cols] = slope.astype(BF16)
                return carry

            lax.fori_loop(0, states // 64, odd_rows, 0)
            r = pl.ds(states, TILE)
            act, slope = gelu_pair(tmp[r] + vec(0, cols))
            last = lax.broadcasted_iota(jnp.int32, act.shape, 0) == TILE - 1
            first = jnp.minimum(seg[s], 1).astype(F32)
            act = jnp.where(last, act * first, 0.0)
            slope = jnp.where(last, slope * first, 0.0)
            odd_act[r, cols] = act
            slope_odd[pl.ds(s * size + states, TILE), cols] = slope.astype(BF16)
            moved = pltpu.roll(odd_act[:, cols], 1, 0)
            taps[pl.ds(s * states, states), cols] = moved[:states].astype(BF16)
            return carry

        lax.fori_loop(0, width // block, odd_columns, 0)

        def even_columns(j, carry, s=s):
            cols = pl.ds(aligned(j, block), block)
            tmp[pl.ds(0, states)] = mat_t(x_even[pl.ds(s * states, states)], w1[cols])

            def even_rows(i, carry):
                r = pl.ds(aligned(i, 64), 64)
                act, slope = gelu_pair(tmp[r] + vec(0, cols))
                out = pl.ds(aligned(i, 64) + s * states, 64)
                taps[out, pl.ds(width + aligned(j, block), block)] = act.astype(BF16)
                slope_even[out, cols] = slope.astype(BF16)
                return carry

            lax.fori_loop(0, states // 64, even_rows, 0)
            return carry

        lax.fori_loop(0, width // block, even_columns, 0)

    for g in second:
        g.after_x()
    for g in third:
        g.after_y()
    for g in second:
        g.finish()
    locals_[3].wait()
    locals_[5].wait()
    locals_[6].wait()

    def state_columns(j, carry):
        cols = pl.ds(aligned(j, block), block)
        tmp[pl.ds(0, rows)] = mat_t(taps[...], w2[cols])

        def state_rows(i, carry):
            r = pl.ds(aligned(i, 64), 64)
            act, slope = gelu_pair(tmp[r] + vec(1, cols))
            block_input[r, cols] = act + pos[r, cols]
            slope_state[r, cols] = slope.astype(BF16)
            return carry

        lax.fori_loop(0, rows // 64, state_rows, 0)
        return carry

    lax.fori_loop(0, width // block, state_columns, 0)
    for g in third:
        g.after_x()
    full = pl.ds(0, width)

    def norm_rows(i, carry):
        r = pl.ds(aligned(i, 32), 32)
        unit, _ = norm_parts(block_input[r])
        normed[r] = (unit * vec(2, full) + vec(3, full)).astype(BF16)
        return carry

    lax.fori_loop(0, rows // 32, norm_rows, 0)
    for g in third:
        g.finish()
    locals_[4].wait()
    group = [m for m in bits_of(at.parts) if m != 2]

    def exchange(array, base):
        held = rows
        for n, mask in enumerate(group):
            copy = pltpu.make_async_remote_copy(
                src_ref=array.at[pl.ds(0, held)],
                dst_ref=array.at[pl.ds(held, held)],
                send_sem=kv_send.at[base + n],
                recv_sem=kv_recv.at[base + n],
                device_id=at.tm_partner(mask),
                device_id_type=MESH,
            )
            copy.start()
            if n + 1 < len(group):
                copy.wait()
                held = 2 * held
            else:
                return copy

    def project(target, first, bias):
        def columns(j, carry):
            cols = pl.ds(aligned(j, block), block)
            part = mat_t(normed[...], wqkv[pl.ds(first + aligned(j, block), block)])
            if bias is not None:
                part = part + vec(bias, cols)
            target[pl.ds(0, rows), cols] = part.astype(BF16)
            return carry

        lax.fori_loop(0, width // block, columns, 0)

    project(keys, width, None)
    key_copy = exchange(keys, 1)
    project(values, 2 * width, 5)
    value_copy = exchange(values, 1 + len(group))
    project(queries, 0, 4)
    key_copy.wait()
    value_copy.wait()
    swap.wait_send()
    for g in groups:
        g.close()


def front(mel, w1_own, vec_own, w2_own, wqkv_own, pos, parts, x_size):
    states = mel.shape[1] - TILE
    rows, width = 2 * states, pos.shape[1]
    every = pos.shape[0]
    shapes = [
        ((parts * w1_own.shape[0], w1_own.shape[1]), BF16),
        ((parts * TILE, vec_own.shape[1]), BF16),
        ((TILE, width), F32),
        ((parts * w2_own.shape[0], w2_own.shape[1]), BF16),
        ((parts * wqkv_own.shape[0], wqkv_own.shape[1]), BF16),
        ((rows, 3 * width), BF16),
        ((rows, 3 * LANES), BF16),
        ((rows + 2 * TILE, 3 * LANES), BF16),
        ((rows, width), BF16),
        ((rows + 2 * TILE, width), BF16),
        ((rows, width), BF16),
        ((rows, width), F32),
        ((rows, width), BF16),
        ((rows, width), BF16),
        ((every, width), BF16),
        ((every, width), BF16),
    ]
    slots = 6 * Gather.slots(parts, x_size)
    return pl.pallas_call(
        functools.partial(front_kernel, states),
        out_shape=[jax.ShapeDtypeStruct(s, d) for s, d in shapes],
        in_specs=[VMEM] * 5 + [ANY],
        out_specs=[VMEM] * len(shapes),
        scratch_shapes=[
            pltpu.VMEM(mel.shape, BF16),
            pltpu.VMEM((states + TILE, width), F32),
            pltpu.VMEM((max(rows, states + TILE), 256), F32),
            pltpu.VMEM((rows, width), F32),
            pltpu.SemaphoreType.DMA((slots,)),
            pltpu.SemaphoreType.DMA((slots,)),
            pltpu.SemaphoreType.DMA((8,)),
            pltpu.SemaphoreType.DMA((8,)),
            pltpu.SemaphoreType.DMA((7,)),
        ],
        compiler_params=pltpu.CompilerParams(
            collective_id=1, has_side_effects=True, vmem_limit_bytes=60 << 20
        ),
        name="front",
    )(mel, w1_own, vec_own, w2_own, wqkv_own, pos)


def reduce_kernel(rows, ahead, source, result, own, landing_y, *refs):
    at = Place()
    chunks = result.shape[0] // rows
    y_bits = list(reversed(bits_of(at.y_size)))
    plane = [("x", b, b) for b in bits_of(at.x_size)]
    plane += [("z", b, b * at.x_size) for b in bits_of(at.z_size)]
    depth = len(plane)
    refs = list(refs)
    sums, landing = [], []
    for k in range(depth):
        sums.append(refs.pop(0))
        landing.append(refs.pop(0))
    sends, receives, local = refs
    coord = {"x": at.x, "z": at.z}
    mine = [(coord[c] // b) % 2 for c, b, _ in plane]
    partner = [at.clip_partner(mask) for _, _, mask in plane]
    y_partner = [at.tm_partner(2 * b) for b in y_bits]
    greet(y_partner + partner)
    tops = len(y_bits)
    held = [0]
    for b in y_bits:
        held.append(held[-1] + b * ((at.y // b) % 2))

    def remote(src, dst, c, slot, device):
        return pltpu.make_async_remote_copy(
            src_ref=src,
            dst_ref=dst,
            send_sem=sends.at[c, slot],
            recv_sem=receives.at[c, slot],
            device_id=device,
            device_id_type=MESH,
        )

    def load(c):
        return pltpu.make_async_copy(
            source.at[pl.ds(held[1], y_bits[0]), pl.ds(c * rows, rows)], own.at[c], local.at[c]
        )

    def y_copy(c, k):
        b = y_bits[k]
        if k == 0:
            away = b * (1 - (at.y // b) % 2)
            src = source.at[pl.ds(away, b), pl.ds(c * rows, rows)]
        else:
            away = b * (1 - (at.y // b) % 2)
            src = own.at[c, pl.ds(away, b)]
        first = sum(y_bits[:k])
        return remote(src, landing_y.at[c, pl.ds(first, b)], c, k, y_partner[k])

    def half(k, bit):
        count = rows >> (k + 1)
        return pl.ds(aligned(bit, count), count)

    def spread(c, k):
        src = sums[k].at[c, half(k, 1 - mine[k])]
        return remote(src, landing[k].at[c], c, tops + k, partner[k])

    def kept(c, k):
        first = c * rows
        for i in range(k + 1):
            first = first + mine[i] * (rows >> (i + 1))
        return pl.ds(pl.multiple_of(first, rows >> (k + 1)), rows >> (k + 1))

    def collect(c, k):
        region = result.at[kept(c, k)]
        return remote(region, region, c, tops + depth + k, partner[k])

    def add(a, b):
        return (a.astype(F32) + b.astype(F32)).astype(BF16)

    def step(stage, c):
        if stage == 0:
            y_copy(c, 0).start()
            load(c).start()
        elif stage <= tops:
            k = stage - 1
            if k == 0:
                load(c).wait()
            y_copy(c, k).wait_recv()
            b = y_bits[k]
            first = sum(y_bits[:k])
            if k == 0:
                total = add(own[c], landing_y[c, pl.ds(first, b)])
            else:
                total = add(own[c, pl.ds(b * ((at.y // b) % 2), b)], landing_y[c, pl.ds(first, b)])
            if k + 1 < tops:
                own[c, pl.ds(0, b)] = total
                y_copy(c, k + 1).start()
            else:
                sums[0][c] = total[0]
                spread(c, 0).start()
        elif stage <= tops + depth:
            k = stage - tops - 1
            spread(c, k).wait_recv()
            total = add(sums[k][c, half(k, mine[k])], landing[k][c])
            if k + 1 < depth:
                sums[k + 1][c] = total
                spread(c, k + 1).start()
            else:
                result[kept(c, k)] = total
                collect(c, k).start()
        else:
            k = depth - 1 - (stage - tops - depth - 1)
            collect(c, k).wait_recv()
            if k > 0:
                collect(c, k - 1).start()

    stages = 1 + tops + 2 * depth
    delays = [0] + [ahead + s for s in range(stages - 1)]
    for time in range(chunks + delays[-1]):
        for stage in range(stages):
            c = time - delays[stage]
            if 0 <= c < chunks:
                step(stage, c)
    for c in range(chunks):
        for k in range(tops):
            y_copy(c, k).wait_send()
        for k in range(depth):
            spread(c, k).wait_send()
            collect(c, k).wait_send()


def reduce_all(source, clips):
    y_size, count, width = source.shape
    x_size = y_size
    plane = len(bits_of(x_size)) + len(bits_of(clips // x_size))
    rows = TILE << plane
    chunks = count // rows
    scratch = [
        pltpu.VMEM((chunks, y_size // 2, rows, width), BF16),
        pltpu.VMEM((chunks, y_size - 1, rows, width), BF16),
    ]
    for k in range(plane):
        scratch.append(pltpu.VMEM((chunks, rows >> k, width), BF16))
        scratch.append(pltpu.VMEM((chunks, rows >> (k + 1), width), BF16))
    slots = len(bits_of(y_size)) + 2 * plane
    scratch += [pltpu.SemaphoreType.DMA((chunks, slots))] * 2
    scratch += [pltpu.SemaphoreType.DMA((chunks,))]
    return pl.pallas_call(
        functools.partial(reduce_kernel, rows, 3),
        out_shape=jax.ShapeDtypeStruct((count, width), BF16),
        in_specs=[ANY],
        out_specs=VMEM,
        scratch_shapes=scratch,
        compiler_params=pltpu.CompilerParams(
            collective_id=2, has_side_effects=True, vmem_limit_bytes=60 << 20
        ),
        name="reduce",
    )(source)


def gather_rows(shard, place, parts):
    pieces = [shard]
    masks = [0]
    for mask in [m for m in bits_of(parts) if m > 1]:
        pieces = pieces + [xor_swap(p, "tm", mask) for p in pieces]
        masks = masks + [m ^ mask for m in masks]
    stack = jnp.stack(pieces)
    other = xor_swap(stack, "tm", 1)
    whole = jnp.zeros((parts,) + shard.shape, shard.dtype)
    for i, mask in enumerate(masks):
        whole = lax.dynamic_update_slice(whole, stack[i][None], (place ^ mask, 0, 0))
        whole = lax.dynamic_update_slice(whole, other[i][None], (place ^ mask ^ 1, 0, 0))
    return whole.reshape(parts * shard.shape[0], shard.shape[1])


def per_device(
    mel_frames,
    lengths,
    conv1_weight,
    conv1_bias,
    conv2_weight,
    conv2_bias,
    ln1_gain,
    ln1_bias,
    qkv_weight,
    q_bias,
    v_bias,
    out_weight,
    out_bias,
    ln2_gain,
    ln2_bias,
    fc1_weight,
    fc1_bias,
    fc2_weight,
    fc2_bias,
    cotangent,
):
    parts = lax.axis_size("tm")
    place = lax.axis_index("tm")
    clips = lax.axis_size("clip")
    y_size = parts // 2
    core, y_place = place % 2, place // 2
    mine = y_place % 2
    frames, mels = mel_frames.shape[1:]
    states, width = cotangent.shape[1:]
    hidden = fc1_weight.shape[1] * parts
    rows = 2 * states
    share = conv1_bias.shape[0]
    size = states + TILE

    w1_own = jnp.pad(conv1_weight, ((0, 0), (0, LANES - mels), (0, 0))).reshape(3 * LANES, share).T
    w2_own = conv2_weight.reshape(3 * width, share).T
    vec_list = [
        conv1_bias, conv2_bias, ln1_gain, ln1_bias, q_bias, v_bias, out_bias, ln2_gain, ln2_bias,
        fc2_bias,
    ]
    vec_own = jnp.concatenate([jnp.stack(vec_list), fc1_bias.reshape(-1, share)], axis=0)
    vec_count = vec_own.shape[0]
    vec_own = jnp.pad(vec_own, ((0, TILE - vec_count), (0, -share % LANES)))

    frame_ids = place * frames + jnp.arange(frames)
    frame_valid = (frame_ids[None, :] < lengths[:, None])[..., None]
    masked = jnp.where(frame_valid, mel_frames, jnp.zeros_like(mel_frames))
    masked = jnp.pad(masked.reshape(2, states, 2, mels), ((0, 0), (0, 0), (0, 0), (0, LANES - mels)))
    masked = masked.reshape(2, states, 2 * LANES)
    up = [(i, i + 1) for i in range(parts - 1)]
    down = [(j, i) for i, j in up]
    before = lax.ppermute(masked[:, states - 1 :], "tm", up)
    after = lax.ppermute(masked[:, :1], "tm", down)
    gap = jnp.zeros((2, TILE - 2, 2 * LANES), BF16)
    mel_ext = jnp.concatenate([masked, after, gap, before], axis=1)
    (
        w1, vec_raw, vecs, w2, wqkv, state_taps, x_even, x_odd, slope_even, slope_odd,
        state_slope, block_input, normed1, queries, keys, values,
    ) = front(
        mel_ext, w1_own, vec_own, w2_own, qkv_weight.T,
        jnp.asarray(positions(states * parts, width)), parts, y_size,
    )
    gain_one, bout, gain_two, shift_two, bfc2 = [vecs[i] for i in (2, 6, 7, 8, 9)]
    bfc1 = vec_raw.reshape(parts, TILE, -1)[:, 10:vec_count, :share].astype(F32).reshape(-1)
    wout = gather_rows(out_weight.T, place, parts)
    wfc1 = gather_rows(fc1_weight.T, place, parts)
    wfc2 = gather_rows(fc2_weight.T, place, parts)

    def swapped(array):
        got = xor_swap(pick(array, 1 - mine), "tm", 2)
        own = pick(array, mine)
        return jnp.where(mine == 0, jnp.stack([own, got]), jnp.stack([got, own]))

    length = pick(lengths, mine)
    cot = swapped(cotangent).reshape(rows, width)
    unit1, scale1 = norm_parts(block_input)
    group = [m for m in bits_of(parts) if m != 2]
    segs = [4 * ((place ^ m) // 4) + 2 * jnp.arange(2) + (place ^ m) % 2 for m in combos(group)]
    segs = jnp.concatenate(segs)
    key_ids = (segs[:, None] * states + jnp.arange(states)[None, :]).reshape(-1)
    key_valid = 2 * key_ids < length
    all_states = key_ids.shape[0]

    def heads(array):
        return array.reshape(-1, HEADS, HEAD_DIM)

    q_h, k_h, v_h = heads(queries), heads(keys), heads(values)
    scores = jnp.einsum("qhd,khd->hqk", q_h, k_h, preferred_element_type=F32) * SCALE
    scores = jnp.where(key_valid, scores, -1e30)
    largest = jnp.max(scores, axis=-1, keepdims=True)
    exponent = jnp.exp(scores - largest)
    probs = (exponent / jnp.sum(exponent, axis=-1, keepdims=True)).astype(BF16)
    attended = jnp.einsum("hqk,khd->qhd", probs, v_h, preferred_element_type=F32)
    attended = attended.reshape(rows, width).astype(BF16)
    middle = block_input + mat_t(attended, wout) + bout
    unit2, scale2 = norm_parts(middle)
    normed2 = (unit2 * gain_two + shift_two).astype(BF16)
    hidden_act, hidden_slope = gelu_pair(mat_t(normed2, wfc1) + bfc1)
    hidden_act = hidden_act.astype(BF16)
    hidden_slope = hidden_slope.astype(BF16)
    out_rows = (middle + mat_t(hidden_act, wfc2) + bfc2).astype(BF16)

    def unswapped(array):
        got = xor_swap(pick(array, 1 - mine), "tm", 2)
        own = pick(array, mine)
        return jnp.where(mine == 0, jnp.stack([own, got]), jnp.stack([got, own]))

    out_states = unswapped(out_rows.reshape(2, states, width))

    def chip_sum(full):
        blocks = full.astype(BF16).reshape(y_size, 2, -1, full.shape[1])
        got = xor_swap(pick(blocks, 1 - core, 1), "tm", 1)
        return (pick(blocks, core, 1).astype(F32) + got.astype(F32)).astype(BF16)

    def chip_grad(grad, acts):
        return chip_sum(mat_l(grad, acts))

    cot_float = cot.astype(F32)
    fc2_parts = [chip_grad(cot, hidden_act[:, i : i + width]) for i in range(0, hidden, width)]
    bfc2_grad = jnp.sum(cot_float, axis=0)
    hidden_grad = (mat(cot, wfc2) * hidden_slope.astype(F32)).astype(BF16)
    fc1_part = chip_grad(hidden_grad, normed2)
    bfc1_grad = jnp.sum(hidden_grad.astype(F32), axis=0)
    normed2_grad = mat(hidden_grad, wfc1)
    gain_two_grad = jnp.sum(normed2_grad * unit2, axis=0)
    shift_two_grad = jnp.sum(normed2_grad, axis=0)
    middle_grad = cot_float + norm_back(normed2_grad, unit2, scale2, gain_two)
    branch_grad = middle_grad.astype(BF16)
    out_part = chip_grad(branch_grad, attended)
    bout_grad = jnp.sum(branch_grad.astype(F32), axis=0)

    attended_grad = mat(branch_grad, wout).astype(BF16)
    a_h = heads(attended_grad)
    row_dot = jnp.sum(a_h.astype(F32) * heads(attended).astype(F32), axis=-1)
    probs_grad = jnp.einsum("qhd,khd->hqk", a_h, v_h, preferred_element_type=F32)
    score_grad = (probs.astype(F32) * (probs_grad - row_dot.T[..., None])).astype(BF16)
    queries_grad = jnp.einsum("hqk,khd->qhd", score_grad, k_h, preferred_element_type=F32)
    queries_grad = (queries_grad * SCALE).reshape(rows, width).astype(BF16)
    keys_term = jnp.einsum("hqk,qhd->khd", score_grad, q_h, preferred_element_type=F32) * SCALE
    values_term = jnp.einsum("hqk,qhd->khd", probs, a_h, preferred_element_type=F32)
    terms = jnp.stack(
        [keys_term.reshape(all_states, width), values_term.reshape(all_states, width)]
    ).astype(BF16)
    for mask in reversed(group):
        half = terms.shape[1] // 2
        got = xor_swap(terms[:, half:], "tm", mask)
        terms = (terms[:, :half].astype(F32) + got.astype(F32)).astype(BF16)
    projected_grad = jnp.concatenate([queries_grad, terms[0], terms[1]], axis=1)
    qkv_part = chip_grad(projected_grad, normed1)
    projected_sum = jnp.sum(projected_grad.astype(F32), axis=0)
    normed1_grad = mat(projected_grad, wqkv)
    gain_one_grad = jnp.sum(normed1_grad * unit1, axis=0)
    shift_one_grad = jnp.sum(normed1_grad, axis=0)
    input_grad = middle_grad + norm_back(normed1_grad, unit1, scale1, gain_one)
    state_grad = (input_grad * state_slope).astype(BF16)
    conv2_parts = [
        chip_grad(state_grad, state_taps[:, i : i + width]) for i in range(0, 3 * width, width)
    ]
    b2_grad = jnp.sum(state_grad.astype(F32), axis=0)
    taps_grad = mat(state_grad, w2)
    prev_grad = taps_grad[:, :width].reshape(2, states, width)
    odd_grad = taps_grad[:, 2 * width :].reshape(2, states, width)
    odd_grad = odd_grad + jnp.pad(prev_grad[:, 1:], ((0, 0), (0, 1), (0, 0)))
    edge_grad = jnp.pad(prev_grad[:, :1], ((0, 0), (TILE - 1, 0), (0, 0)))
    odd_grad = jnp.concatenate([odd_grad, edge_grad], axis=1).reshape(2 * size, width)
    odd_grad = (odd_grad * slope_odd).astype(BF16)
    even_grad = (taps_grad[:, width : 2 * width] * slope_even).astype(BF16)
    b1_grad = jnp.sum(even_grad.astype(F32), axis=0) + jnp.sum(odd_grad.astype(F32), axis=0)
    conv1_part = chip_sum(mat_l(even_grad, x_even) + mat_l(odd_grad, x_odd))
    half = conv1_part.shape[1] // 2
    conv1_part = jnp.concatenate([conv1_part[:, :half], conv1_part[:, half:]], axis=2)

    vec_grads = [
        b1_grad, b2_grad, gain_one_grad, shift_one_grad, projected_sum[:width],
        projected_sum[2 * width :], bout_grad, gain_two_grad, shift_two_grad, bfc2_grad,
    ]
    vec_part = jnp.stack([v.reshape(parts, share) for v in vec_grads], axis=1)
    vec_part = jnp.concatenate([vec_part, bfc1_grad.reshape(parts, -1, share)], axis=1)
    vec_part = vec_part.reshape(y_size, 2, vec_count, share)
    got = xor_swap(pick(vec_part, 1 - core, 1), "tm", 1)
    vec_part = (pick(vec_part, core, 1) + got).astype(BF16)
    vec_part = jnp.pad(vec_part, ((0, 0), (0, TILE - vec_count), (0, width - share)))
    pieces = fc2_parts + [fc1_part, out_part, qkv_part] + conv2_parts + [conv1_part, vec_part]
    sizes = [p.shape[1] for p in pieces]
    packed = jnp.concatenate(pieces, axis=1)
    step = TILE * clips
    packed = jnp.pad(packed, ((0, 0), (0, -packed.shape[1] % step), (0, 0)))
    summed = reduce_all(packed, clips)
    ends = [sum(sizes[: i + 1]) for i in range(len(sizes))]
    sums = [summed[e - s : e].astype(F32) for e, s in zip(ends, sizes)]
    fc2_sum = jnp.concatenate([s.T for s in sums[: len(fc2_parts)]], axis=0)
    fc1_sum, out_sum, qkv_sum = sums[len(fc2_parts) : len(fc2_parts) + 3]
    conv2_sum = jnp.stack([s.T for s in sums[-5:-2]])
    conv1_sum = sums[-2]
    conv1_sum = jnp.concatenate([conv1_sum[:, : 3 * LANES], conv1_sum[:, 3 * LANES :]], axis=0)
    conv1_sum = conv1_sum.T.reshape(3, LANES, share)[:, :mels]
    vec_sum = sums[-1][:vec_count, :share]

    even_back = mat(even_grad, w1).reshape(2, states, 3 * LANES)
    even_back = jnp.pad(even_back, ((0, 0), (0, TILE), (0, 0)))
    odd_back = mat(odd_grad, w1).reshape(2, size, 3 * LANES)
    even_mel = even_back[..., LANES : 2 * LANES] + odd_back[..., :LANES]
    even_mel = even_mel + jnp.roll(odd_back[..., 2 * LANES :], 1, axis=1)
    odd_mel = jnp.roll(even_back[..., :LANES], -1, axis=1)
    odd_mel = odd_mel + even_back[..., 2 * LANES :] + odd_back[..., LANES : 2 * LANES]
    mel_back = unswapped(jnp.stack([even_mel[..., :mels], odd_mel[..., :mels]], axis=2))
    from_before = lax.ppermute(mel_back[:, states], "tm", up)
    from_after = lax.ppermute(mel_back[:, size - 1], "tm", down)
    mel_back = mel_back[:, :states].at[:, 0].add(from_before).at[:, -1].add(from_after)
    mel_back = mel_back.reshape(2, frames, mels)
    mel_grad = jnp.where(frame_valid, mel_back, 0.0).astype(BF16)

    return (
        out_states,
        mel_grad,
        conv1_sum,
        vec_sum[0],
        conv2_sum,
        vec_sum[1],
        vec_sum[2],
        vec_sum[3],
        qkv_sum.T,
        vec_sum[4],
        vec_sum[5],
        out_sum.T,
        vec_sum[6],
        vec_sum[7],
        vec_sum[8],
        fc1_sum.T,
        vec_sum[10:].reshape(-1),
        fc2_sum,
        vec_sum[9],
    )


def solution(mesh):
    return jax.shard_map(
        per_device,
        mesh=mesh,
        in_specs=(
            P("clip", "tm", None),
            P("clip"),
            P(None, None, "tm"),
            P("tm"),
            P(None, None, "tm"),
            P("tm"),
            P("tm"),
            P("tm"),
            P(None, "tm"),
            P("tm"),
            P("tm"),
            P(None, "tm"),
            P("tm"),
            P("tm"),
            P("tm"),
            P(None, "tm"),
            P("tm"),
            P(None, "tm"),
            P("tm"),
            P("clip", "tm", None),
        ),
        out_specs=(
            P("clip", "tm", None),
            P("clip", "tm", None),
            P(None, None, "tm"),
            P("tm"),
            P(None, None, "tm"),
            P("tm"),
            P("tm"),
            P("tm"),
            P(None, "tm"),
            P("tm"),
            P("tm"),
            P(None, "tm"),
            P("tm"),
            P("tm"),
            P("tm"),
            P(None, "tm"),
            P("tm"),
            P(None, "tm"),
            P("tm"),
        ),
        check_vma=False,
    )
```

time: 658 us -> 527 us (0.80)
  waiting for transfers between devices: 242 us -> 2.78 us
  Pallas kernels: 0 us -> 230 us
  local copies, waits for them, and re-layouts: 152 us -> 80.3 us
  matrix products: 142 us -> 106 us
  starting transfers between devices: 33.5 us -> 22.4 us
    ppermute x45 -> x22, waiting for transfers between devices: 242 us -> 0.58 us  [xor_swap(): return lax.ppermute(array, axis, [(i, i ^ mask) for i in range(size)])]
    pallas_call x0 -> x2, Pallas kernels: none -> 230 us  [the longest x1 132 us: reduce_all(): pl.pallas_call(functools.partial(reduce_kernel, rows, 3), out_shape=jax.S...]
    dynamic_slice x9 -> x2, local copies, waits for them, and re-layouts: 26.1 us -> 1.39 us  [pick(): return lax.dynamic_index_in_dim(array, index, axis=axis, keepdims=False)]
    dot_general x12, matrix products: 42.2 us -> 20.2 us  [mat_l(): lax.dot_general(a, b, (((0,), (0,)), ((), ())), preferred_element_type=F32)]
    unnamed x6 -> x12, other arithmetic: 0.09 us -> 21.7 us
    reshape x24 -> x7, local copies, waits for them, and re-layouts: 24.5 us -> 4.36 us  [the longest x1 1.07 us: per_device(): conv1_sum = conv1_sum.T.reshape(3, LANES, share)[:, :mels]]
    ppermute x45 -> x22, starting transfers between devices: 33.5 us -> 15.2 us  [xor_swap(): return lax.ppermute(array, axis, [(i, i ^ mask) for i in range(size)])]
    dot_general x6 -> x3, matrix products: 30 us -> 16 us  [mat_t(): lax.dot_general(a, b, (((1,), (1,)), ((), ())), preferred_element_type=F32)]
  transfers between devices with their start and end apart: 45 -> 26, of which waited for: 17 -> 3; matrix products, arithmetic and copies ran while one was open for 38% -> 30% of each run, Pallas kernels for 0% -> 19%
where the time goes in v2:
time: 527 us; the launch traced here: 517 us
  Pallas kernels  230 us (44%)
  matrix products  106 us (20%)
  local copies, waits for them, and re-layouts  80.3 us (15%)
  other arithmetic  73.1 us (14%)
  starting transfers between devices  22.4 us (4%)
    pallas_call x1, Pallas kernels, reduce_all(): pl.pallas_call(functools.partial(reduce_kernel, rows, 3), out_shape=jax.S...  132 us
    pallas_call x1, Pallas kernels, front(): pl.pallas_call(functools.partial(front_kernel, states), out_shape=[jax.Sh...  97.4 us
    unnamed x12, other arithmetic  21.7 us
    dot_general x7, matrix products, mat(): return jnp.dot(a, b, preferred_element_type=F32)  21.3 us
    dot_general x12, matrix products, mat_l(): lax.dot_general(a, b, (((0,), (0,)), ((), ())), preferred_element_type=F32)  20.2 us
    dot_general x3, matrix products, mat_t(): lax.dot_general(a, b, (((1,), (1,)), ((), ())), preferred_element_type=F32)  16 us
    unnamed x176, local copies, waits for them, and re-layouts  15.5 us
    ppermute x22, starting transfers between devices, xor_swap(): return lax.ppermute(array, axis, [(i, i ^ mask) for i in range(size)])  15.2 us
  transfers between devices with their start and end apart: 26, of which 3 were waited for; matrix products, arithmetic and copies ran while one was open for 30% of the time, Pallas kernels for 19%

profile of v2, /device:TPU:0, one launch (start us, length us, event | category | flops | bytes accessed | tf_op | source)
XLA Modules:
  0.0 517.0 jit_solution(9722351198810728231)
XLA Ops:
  3.7 2.4 collective-permute-start.1
  7.3 4.9 collective-permute-start.2
  13.7 2.0 collective-permute-start.6
  20.9 3.0 broadcast_in_dim.64
  24.5 2.5 constant_dynamic-update-slice_fusion.3
  31.4 97.4 %front.1 = (bf16[768,384]{1,0:T(8,128)(2,1)}, bf16[64,256]{1,0:T(8,128)(2,1)}, f32[16,768]{1,0:T(8,128)}, bf16[768,2304]{1,0:T(8,128)(2,1)}, bf16[2304,768]{1,0:...) custom-call(bf16[2,272,256]{2,1,0:T(8,128)(2,1)} %pad_maximum_fusion, ...), custom_call_target="tpu_custom_call" | custom-call | tf_op jit(solution)/shard_map/front/pallas_call | solution.py:505
  128.8 2.7 copy.59
  134.5 14.2 %fusion.65 = (f32[12,512]{1,0:T(8,128)}, f32[12,512,1024]{2,1,0:T(8,128)}) fusion(pred[1024]{0:T(1024)(128)(4,1)S(1)} %lt.114, bf16[512,12,64]{0,2,1:T(8,128)(2,1)} %bitcast.299, bf16[1024,12,64]{0,2,1:T(8,128)(2,1)S(1)} %bitcast.288), kind=kOutput, calls=%fused_computation.226 | convolution fusion | flops 830473216 | bytes 27550720 | tf_op jit(solution)/shard_map/sub | solution.py:785
  148.7 10.2 %divide_convert_fusion = bf16[12,512,1024]{2,1,0:T(8,128)(2,1)S(1)} fusion(f32[12,512,1024]{2,1,0:T(8,128)} %get-tuple-element.179, f32[12,512]{1,0:T(8,128)} %get-tuple-element.178), kind=kLoop, calls=%fused_computation.2 | loop fusion | flops 12582912 | bytes 37773312 | tf_op jit(solution)/shard_map/convert_element_type | solution.py:786
  158.9 7.4 %convolution_convert_fusion.12 = bf16[12,64,512]{2,1,0:T(8,128)(2,1)} fusion(bf16[1024,12,64]{0,2,1:T(8,128)(2,1)} %bitcast.282, bf16[12,512,1024]{2,1,0:T(8,128)(2,1)S(1)} %divide_convert_fusion), kind=kOutput, calls=%fused_computation.80 | convolution fusion | flops 805699584 | bytes 14942208 | tf_op jit(solution)/shard_map/hqk,khd->qhd/dot_general | solution.py:787
  170.8 3.2 pad_maximum_fusion
  184.6 2.2 fusion.66
  187.2 2.1 pad_maximum_fusion.1
  193.6 8.3 %multiply_convert_fusion.2 = (bf16[512,3072]{1,0:T(8,128)(2,1)}, f32[512,3072]{1,0:T(8,128)S(1)}) fusion(f32[3072]{0:T(1024)S(1)} %copy-done.60, bf16[3072,768]{1,0:T(8,128)(2,1)S(1)} %bitcast.297, f32[512,768]{1,0:T(8,128)S(1)} %get-tuple-element.181, f32[768]{0:T(1024)S(1)} %get-tuple-element.123, f32[768]{0:T(1024)S(1)} %get-tuple-element.124, ...), kind=kOutput, calls=%fused_computation.19 | convolution fusion | flops 2454061056 | bytes 15751168 | tf_op jit(solution)/shard_map/dot_general | solution.py:94
  203.0 2.4 constant_dynamic-update-slice_fusion.2
  206.5 9.8 %convert_reduce_fusion = (f32[3072]{0:T(1024)}, bf16[512,3072]{1,0:T(8,128)(2,1)S(1)}) fusion(f32[512,3072]{1,0:T(8,128)S(1)} %get-tuple-element.183, f32[3072]{0:T(1024)S(1)} %copy-done.60, bf16[512,768]{1,0:T(8,128)(2,1)S(1)} %bitcast.311, bf16[768,3072]{1,0:T(8,128)(2,1)} %bitcast.26), kind=kOutput, calls=%fused_computation.17 | convolution fusion | flops 2463101952 | bytes 14966784 | tf_op jit(solution)/shard_map/dot_general | solution.py:90
  216.3 3.5 multiply_reduce_fusion
  221.6 2.1 convolution_convert_fusion.11
  224.0 8.3 %convolution_convert_fusion.2 = bf16[12,64,1024]{2,1,0:T(8,128)(2,1)} fusion(bf16[512,12,64]{0,2,1:T(8,128)(2,1)S(1)} %bitcast.279, bf16[12,512,1024]{2,1,0:T(8,128)(2,1)} %copy-done), kind=kOutput, calls=%fused_computation.40 | convolution fusion | flops 806092800 | bytes 14942208 | tf_op jit(solution)/shard_map/hqk,qhd->khd/dot_general | solution.py:834
  232.5 8.1 %multiply_convert_fusion = bf16[12,512,1024]{2,1,0:T(8,128)(2,1)S(1)} fusion(bf16[12,512,1024]{2,1,0:T(8,128)(2,1)} %copy-done, f32[12,512]{1,0:T(8,128)S(1)} %bitcast.344, bf16[512,12,64]{0,2,1:T(8,128)(2,1)} %bitcast.281, bf16[1024,12,64]{0,2,1:T(8,128)(2,1)} %bitcast.283), kind=kOutput, calls=%fused_computation.1 | convolution fusion | flops 830472192 | bytes 27549696 | tf_op jit(solution)/shard_map/qhd,khd->hqk/dot_general | solution.py:829
  240.7 4.6 multiply_convert_fusion.3
  245.2 6.3 %multiply_convert_fusion.5 = bf16[12,64,512]{2,1,0:T(8,128)(2,1)} fusion(bf16[1024,12,64]{0,2,1:T(8,128)(2,1)} %bitcast.289, bf16[12,512,1024]{2,1,0:T(8,128)(2,1)S(1)} %multiply_convert_fusion), kind=kOutput, calls=%fused_computation.60 | convolution fusion | flops 806092800 | bytes 14942208 | tf_op jit(solution)/shard_map/hqk,khd->qhd/dot_general | solution.py:831
  251.5 2.2 convolution_convert_fusion.10
  253.8 2.4 convolution_convert_fusion.9
  259.6 4.9 convolution_convert_fusion.1
  265.3 5.5 %add_convert_fusion.1 = bf16[512,768]{1,0:T(8,128)(2,1)S(1)} fusion(f32[512,768]{1,0:T(8,128)S(1)} %copy-done.14, bf16[512,3072]{1,0:T(8,128)(2,1)S(1)} %copy-done.80, bf16[768,3072]{1,0:T(8,128)(2,1)} %bitcast.26, f32[768]{0:T(1024)S(1)} %get-tuple-element.122), kind=kOutput, calls=%fused_computation.64 | convolution fusion | flops 2417098752 | bytes 10226688 | tf_op jit(solution)/shard_map/dot_general | solution.py:94
  281.9 3.4 dynamic-slice_bitcast_fusion
  285.7 2.2 maximum_select_fusion
  288.1 2.2 fusion.34
  290.5 2.0 fusion.35
  292.5 2.0 fusion.36
  295.6 2.2 add_convert_fusion
  299.4 2.6 multiply_reduce_fusion.1
  304.3 2.0 fusion.67
  316.8 2.0 convolution_convert_fusion
  325.4 2.2 convolution_convert_fusion.3
  330.3 2.1 collective-permute-start.12
  336.6 2.9 collective-permute-start.24
  342.7 4.5 fusion.13
  347.2 2.0 fusion.38
  349.2 3.3 fusion.14
  352.5 2.1 fusion.39
  357.9 7.9 %pad.43.source = bf16[2,3072,768]{2,1,0:T(8,128)(2,1)} pad(bf16[2,2992,768]{2,1,0:T(8,128)(2,1)} %pad_dynamic-update-slice_fusion, bf16[]{:T(256)} %constant.232.clone.1), padding=0_0x0_80x0_0 | pad | bytes 18628610 | tf_op jit(solution)/shard_map/jit(_pad)/pad | solution.py:881
  365.8 132.2 %reduce.16 = bf16[3072,768]{1,0:T(8,128)(2,1)} custom-call(bf16[2,3072,768]{2,1,0:T(8,128)(2,1)} %pad.43.source), custom_call_target="tpu_custom_call" | custom-call | tf_op jit(solution)/shard_map/reduce/pallas_call | solution.py:666
  499.7 2.9 slice_bitcast_fusion.5
  502.6 2.5 convert_bitcast_fusion.1
  509.8 1.9 copy.96
  512.5 2.4 maximum_convert_fusion.1
  (367 shorter events, 102.7 us)
Async XLA Ops:
  0.7 11.6 %copy-start.27 = (bf16[768,768]{1,0:T(8,128)(2,1)S(1)}, bf16[768,768]{1,0:T(8,128)(2,1)}, u32[]{:S(2)}) copy-start(bf16[768,768]{1,0:T(8,128)(2,1)} %param.40) | copy-start | bytes 3538948
  0.7 15.1 %copy-start.50 = (bf16[3,80,192]{2,1,0:T(8,128)(2,1)S(1)}, bf16[3,80,192]{2,1,0:T(8,128)(2,1)}, u32[]{:S(2)}) copy-start(bf16[3,80,192]{2,1,0:T(8,128)(2,1)} %param.27) | copy-start | bytes 276484
  2.6 13.9 %copy-start.70 = (bf16[192]{0:T(256)(128)(2,1)S(1)}, bf16[192]{0:T(256)(128)(2,1)}, u32[]{:S(2)}) copy-start(bf16[192]{0:T(256)(128)(2,1)} %param.28) | copy-start | bytes 1156
  2.6 13.9 %copy-start.71 = (bf16[192]{0:T(256)(128)(2,1)S(1)}, bf16[192]{0:T(256)(128)(2,1)}, u32[]{:S(2)}) copy-start(bf16[192]{0:T(256)(128)(2,1)} %param.30) | copy-start | bytes 1156
  2.6 14.0 %copy-start.72 = (bf16[192]{0:T(256)(128)(2,1)S(1)}, bf16[192]{0:T(256)(128)(2,1)}, u32[]{:S(2)}) copy-start(bf16[192]{0:T(256)(128)(2,1)} %param.31) | copy-start | bytes 1156
  2.6 14.0 %copy-start.73 = (bf16[192]{0:T(256)(128)(2,1)S(1)}, bf16[192]{0:T(256)(128)(2,1)}, u32[]{:S(2)}) copy-start(bf16[192]{0:T(256)(128)(2,1)} %param.32) | copy-start | bytes 1156
  2.6 14.0 %copy-start.74 = (bf16[192]{0:T(256)(128)(2,1)S(1)}, bf16[192]{0:T(256)(128)(2,1)}, u32[]{:S(2)}) copy-start(bf16[192]{0:T(256)(128)(2,1)} %param.34) | copy-start | bytes 1156
  2.7 14.0 %copy-start.75 = (bf16[192]{0:T(256)(128)(2,1)S(1)}, bf16[192]{0:T(256)(128)(2,1)}, u32[]{:S(2)}) copy-start(bf16[192]{0:T(256)(128)(2,1)} %param.35) | copy-start | bytes 1156
  2.7 14.0 %copy-start.76 = (bf16[192]{0:T(256)(128)(2,1)S(1)}, bf16[192]{0:T(256)(128)(2,1)}, u32[]{:S(2)}) copy-start(bf16[192]{0:T(256)(128)(2,1)} %param.37) | copy-start | bytes 1156
  2.7 14.0 %copy-start.77 = (bf16[192]{0:T(256)(128)(2,1)S(1)}, bf16[192]{0:T(256)(128)(2,1)}, u32[]{:S(2)}) copy-start(bf16[192]{0:T(256)(128)(2,1)} %param.38) | copy-start | bytes 1156
  2.7 14.0 %copy-start.65 = (s32[2]{0:T(128)S(1)}, s32[2]{0:T(128)}, u32[]{:S(2)}) copy-start(s32[2]{0:T(128)} %param.26) | copy-start | bytes 28
  3.5 15.0 %copy-start.40 = (bf16[768,192]{0,1:T(8,128)(2,1)S(1)}, bf16[768,192]{0,1:T(8,128)(2,1)}, u32[]{:S(2)}) copy-start(bf16[768,192]{0,1:T(8,128)(2,1)} %param.36) | copy-start | bytes 884740
  3.7 26.8 %collective-permute-start.1 = (bf16[2,1,256]{2,1,0:T(2,128)(2,1)S(1)}, bf16[2,1,256]{2,1,0:T(2,128)(2,1)S(1)}, u32[]{:S(2)}, u32[]{:S(2)}) collective-permute-start(bf16[2,1,256]{2,1,0:T(2,128)(2,1)S(1)} %get-tuple-element.165), channel_id=1, source_target_pairs={{0,1},{1,2},{2,3},{4,5},{5,6},{6,7},{8,9},{9,10},{10,11},{12,13},{... | collective-permute-start | bytes 3080 | tf_op jit(solution)/shard_map/ppermute | solution.py:746
  6.0 24.5 %collective-permute-start = (bf16[2,1,256]{2,1,0:T(2,128)(2,1)S(1)}, bf16[2,1,256]{2,1,0:T(2,128)(2,1)S(1)}, u32[]{:S(2)}, u32[]{:S(2)}) collective-permute-start(bf16[2,1,256]{2,1,0:T(2,128)(2,1)S(1)} %get-tuple-element.164), channel_id=1, source_target_pairs={{1,0},{2,1},{3,2},{5,4},{6,5},{7,6},{9,8},{10,9},{11,10},{13,12},{... | collective-permute-start | bytes 3080 | tf_op jit(solution)/shard_map/ppermute | solution.py:747
  7.3 161.4 %collective-permute-start.2 = (bf16[192,768]{1,0:T(8,128)(2,1)}, bf16[192,768]{1,0:T(8,128)(2,1)}, u32[]{:S(2)}, u32[]{:S(2)}) collective-permute-start(bf16[192,768]{1,0:T(8,128)(2,1)} %bitcast.333), channel_id=1, source_target_pairs={{0,2},{1,3},{2,0},{3,1},{4,6},{5,7},{6,4},{7,5},{8,10},{9,11},{10,... | collective-permute-start | bytes 884744 | tf_op jit(solution)/shard_map/ppermute | solution.py:26
  13.7 157.1 %collective-permute-start.4 = (bf16[768,768]{1,0:T(8,128)(2,1)}, bf16[768,768]{1,0:T(8,128)(2,1)}, u32[]{:S(2)}, u32[]{:S(2)}) collective-permute-start(bf16[768,768]{1,0:T(8,128)(2,1)} %bitcast.16), channel_id=1, source_target_pairs={{0,2},{1,3},{2,0},{3,1},{4,6},{5,7},{6,4},{7,5},{8,10},{9,11},{10,... | collective-permute-start | bytes 3538952 | tf_op jit(solution)/shard_map/ppermute | solution.py:26
  13.7 173.4 %collective-permute-start.6 = (bf16[192,3072]{1,0:T(8,128)(2,1)}, bf16[192,3072]{1,0:T(8,128)(2,1)}, u32[]{:S(2)}, u32[]{:S(2)}) collective-permute-start(bf16[192,3072]{1,0:T(8,128)(2,1)} %bitcast.22), channel_id=1, source_target_pairs={{0,2},{1,3},{2,0},{3,1},{4,6},{5,7},{6,4},{7,5},{8,10},{9,11},{10,... | collective-permute-start | bytes 3538952 | tf_op jit(solution)/shard_map/ppermute | solution.py:26
  30.4 146.8 %collective-permute-start.9 = (bf16[256,768]{1,0:T(8,128)(2,1)}, bf16[256,768]{1,0:T(8,128)(2,1)}, u32[]{:S(2)}, u32[]{:S(2)}) collective-permute-start(bf16[256,768]{1,0:T(8,128)(2,1)} %get-tuple-element.152), channel_id=1, source_target_pairs={{0,2},{1,3},{2,0},{3,1},{4,6},{5,7},{6,4},{7,5},{8,10},{9,11},{10,... | collective-permute-start | bytes 1179656 | tf_op jit(solution)/shard_map/ppermute | solution.py:26
  134.3 14.4 %copy-start.12 = (bf16[1024,768]{0,1:T(8,128)(2,1)}, bf16[1024,768]{0,1:T(8,128)(2,1)S(1)}, u32[]{:S(2)}) copy-start(bf16[1024,768]{0,1:T(8,128)(2,1)S(1)} %copy.61) | copy-start | bytes 4718596
  134.5 31.8 %copy-start.53 = (f32[512]{0:T(512)}, f32[512]{0:T(512)S(1)}, u32[]{:S(2)}) copy-start(f32[512]{0:T(512)S(1)} %broadcast_multiply_fusion.1) | copy-start | bytes 6148
  170.6 8.7 %collective-permute-start.3 = (bf16[2,192,768]{2,1,0:T(8,128)(2,1)}, bf16[2,192,768]{2,1,0:T(8,128)(2,1)}, u32[]{:S(2)}, u32[]{:S(2)}) collective-permute-start(bf16[2,192,768]{2,1,0:T(8,128)(2,1)} %pad_maximum_fusion.4), channel_id=1, source_target_pairs={{0,1},{1,0},{2,3},{3,2},{4,5},{5,4},{6,7},{7,6},{8,9},{9,8},{10,11... | collective-permute-start | bytes 1769480 | tf_op jit(solution)/shard_map/ppermute | solution.py:26
  174.0 15.4 %collective-permute-start.5 = (bf16[2,768,768]{2,1,0:T(8,128)(2,1)}, bf16[2,768,768]{2,1,0:T(8,128)(2,1)}, u32[]{:S(2)}, u32[]{:S(2)}) collective-permute-start(bf16[2,768,768]{2,1,0:T(8,128)(2,1)} %pad_maximum_fusion), channel_id=1, source_target_pairs={{0,1},{1,0},{2,3},{3,2},{4,5},{5,4},{6,7},{7,6},{8,9},{9,8},{10,11... | collective-permute-start | bytes 7077896 | tf_op jit(solution)/shard_map/ppermute | solution.py:26
  178.5 41.3 %copy-start.21 = (bf16[2,256,768]{2,1,0:T(8,128)(2,1)}, bf16[2,256,768]{2,1,0:T(8,128)(2,1)S(1)}, u32[]{:S(2)}) copy-start(bf16[2,256,768]{2,1,0:T(8,128)(2,1)S(1)} %get-tuple-element.127) | copy-start | bytes 2359300
  186.8 33.0 %copy-start.13 = (f32[512,768]{1,0:T(8,128)}, f32[512,768]{1,0:T(8,128)S(1)}, u32[]{:S(2)}) copy-start(f32[512,768]{1,0:T(8,128)S(1)} %get-tuple-element.181) | copy-start | bytes 4718596
  189.2 12.7 %collective-permute-start.7 = (bf16[2,192,3072]{2,1,0:T(8,128)(2,1)S(1)}, bf16[2,192,3072]{2,1,0:T(8,128)(2,1)S(1)}, u32[]{:S(2)}, u32[]{:S(2)}) collective-permute-start(bf16[2,192,3072]{2,1,0:T(8,128)(2,1)S(1)} %pad_maximum_fusion.1), channel_id=1, source_target_pairs={{0,1},{1,0},{2,3},{3,2},{4,5},{5,4},{6,7},{7,6},{8,9},{9,8},{10,11... | collective-permute-start | bytes 7077896 | tf_op jit(solution)/shard_map/ppermute | solution.py:26
  253.8 20.3 %copy-start.38 = (bf16[768,768]{1,0:T(8,128)(2,1)}, bf16[768,768]{1,0:T(8,128)(2,1)S(1)}, u32[]{:S(2)}) copy-start(bf16[768,768]{1,0:T(8,128)(2,1)S(1)} %convolution_convert_fusion.10) | copy-start | bytes 3538948
  256.3 18.7 %copy-start.36 = (bf16[768,768]{1,0:T(8,128)(2,1)}, bf16[768,768]{1,0:T(8,128)(2,1)S(1)}, u32[]{:S(2)}) copy-start(bf16[768,768]{1,0:T(8,128)(2,1)S(1)} %convolution_convert_fusion.9) | copy-start | bytes 3538948
  257.2 19.2 %copy-start.34 = (bf16[768,768]{1,0:T(8,128)(2,1)}, bf16[768,768]{1,0:T(8,128)(2,1)S(1)}, u32[]{:S(2)}) copy-start(bf16[768,768]{1,0:T(8,128)(2,1)S(1)} %convolution_convert_fusion.8) | copy-start | bytes 3538948
  259.5 17.8 %copy-start.32 = (bf16[768,768]{1,0:T(8,128)(2,1)}, bf16[768,768]{1,0:T(8,128)(2,1)S(1)}, u32[]{:S(2)}) copy-start(bf16[768,768]{1,0:T(8,128)(2,1)S(1)} %convolution_convert_fusion.7) | copy-start | bytes 3538948
  265.3 12.9 %copy-start.15 = (bf16[768,768]{1,0:T(8,128)(2,1)}, bf16[768,768]{1,0:T(8,128)(2,1)S(1)}, u32[]{:S(2)}) copy-start(bf16[768,768]{1,0:T(8,128)(2,1)S(1)} %convolution_convert_fusion.6) | copy-start | bytes 3538948
  271.7 13.6 %collective-permute-start.8 = (bf16[256,768]{1,0:T(8,128)(2,1)}, bf16[256,768]{1,0:T(8,128)(2,1)}, u32[]{:S(2)}, u32[]{:S(2)}) collective-permute-start(bf16[256,768]{1,0:T(8,128)(2,1)} %get-tuple-element.155), channel_id=1, source_target_pairs={{0,2},{1,3},{2,0},{3,1},{4,6},{5,7},{6,4},{7,5},{8,10},{9,11},{10,... | collective-permute-start | bytes 1179656 | tf_op jit(solution)/shard_map/ppermute | solution.py:26
  273.7 21.9 %collective-permute-start.10 = (bf16[2,512,768]{1,2,0:T(8,128)(2,1)}, bf16[2,512,768]{1,2,0:T(8,128)(2,1)}, u32[]{:S(2)}, u32[]{:S(2)}) collective-permute-start(bf16[2,512,768]{1,2,0:T(8,128)(2,1)} %pad_maximum_fusion.3), channel_id=1, source_target_pairs={{0,1},{1,0},{2,3},{3,2},{4,5},{5,4},{6,7},{7,6},{8,9},{9,8},{10,11... | collective-permute-start | bytes 4718600 | tf_op jit(solution)/shard_map/ppermute | solution.py:26
  274.9 13.0 %collective-permute-start.14 = (bf16[2,192,768]{2,1,0:T(8,128)(2,1)}, bf16[2,192,768]{2,1,0:T(8,128)(2,1)}, u32[]{:S(2)}, u32[]{:S(2)}) collective-permute-start(bf16[2,192,768]{2,1,0:T(8,128)(2,1)} %dynamic-slice_bitcast_fusion.9), channel_id=1, source_target_pairs={{0,1},{1,0},{2,3},{3,2},{4,5},{5,4},{6,7},{7,6},{8,9},{9,8},{10,11... | collective-permute-start | bytes 1769480 | tf_op jit(solution)/shard_map/ppermute | solution.py:26
  276.0 14.2 %collective-permute-start.15 = (bf16[2,192,768]{2,1,0:T(8,128)(2,1)}, bf16[2,192,768]{2,1,0:T(8,128)(2,1)}, u32[]{:S(2)}, u32[]{:S(2)}) collective-permute-start(bf16[2,192,768]{2,1,0:T(8,128)(2,1)} %dynamic-slice_bitcast_fusion.8), channel_id=1, source_target_pairs={{0,1},{1,0},{2,3},{3,2},{4,5},{5,4},{6,7},{7,6},{8,9},{9,8},{10,11... | collective-permute-start | bytes 1769480 | tf_op jit(solution)/shard_map/ppermute | solution.py:26
  277.2 15.3 %collective-permute-start.16 = (bf16[2,192,768]{2,1,0:T(8,128)(2,1)}, bf16[2,192,768]{2,1,0:T(8,128)(2,1)}, u32[]{:S(2)}, u32[]{:S(2)}) collective-permute-start(bf16[2,192,768]{2,1,0:T(8,128)(2,1)} %dynamic-slice_bitcast_fusion.7), channel_id=1, source_target_pairs={{0,1},{1,0},{2,3},{3,2},{4,5},{5,4},{6,7},{7,6},{8,9},{9,8},{10,11... | collective-permute-start | bytes 1769480 | tf_op jit(solution)/shard_map/ppermute | solution.py:26
  285.3 9.3 %collective-permute-start.17 = (bf16[2,192,768]{2,1,0:T(8,128)(2,1)S(1)}, bf16[2,192,768]{2,1,0:T(8,128)(2,1)S(1)}, u32[]{:S(2)}, u32[]{:S(2)}) collective-permute-start(bf16[2,192,768]{2,1,0:T(8,128)(2,1)S(1)} %copy-done.48), channel_id=1, source_target_pairs={{0,1},{1,0},{2,3},{3,2},{4,5},{5,4},{6,7},{7,6},{8,9},{9,8},{10,11... | collective-permute-start | bytes 1769480 | tf_op jit(solution)/shard_map/ppermute | solution.py:26
  287.9 54.6 %collective-permute-start.18 = (bf16[2,768,768]{2,1,0:T(8,128)(2,1)}, bf16[2,768,768]{2,1,0:T(8,128)(2,1)}, u32[]{:S(2)}, u32[]{:S(2)}) collective-permute-start(bf16[2,768,768]{2,1,0:T(8,128)(2,1)} %dynamic-slice_bitcast_fusion), channel_id=1, source_target_pairs={{0,1},{1,0},{2,3},{3,2},{4,5},{5,4},{6,7},{7,6},{8,9},{9,8},{10,11... | collective-permute-start | bytes 7077896 | tf_op jit(solution)/shard_map/ppermute | solution.py:26
  290.2 56.9 %collective-permute-start.19 = (bf16[2,192,768]{2,1,0:T(8,128)(2,1)}, bf16[2,192,768]{2,1,0:T(8,128)(2,1)}, u32[]{:S(2)}, u32[]{:S(2)}) collective-permute-start(bf16[2,192,768]{2,1,0:T(8,128)(2,1)} %dynamic-slice_bitcast_fusion.5), channel_id=1, source_target_pairs={{0,1},{1,0},{2,3},{3,2},{4,5},{5,4},{6,7},{7,6},{8,9},{9,8},{10,11... | collective-permute-start | bytes 1769480 | tf_op jit(solution)/shard_map/ppermute | solution.py:26
  315.7 12.8 %collective-permute-start.11 = (f32[272,2,80]{2,1,0:T(2,128)}, f32[272,2,80]{2,1,0:T(2,128)}, u32[]{:S(2)}, u32[]{:S(2)}) collective-permute-start(f32[272,2,80]{2,1,0:T(2,128)} %get-tuple-element.159), channel_id=1, source_target_pairs={{0,2},{1,3},{2,0},{3,1},{4,6},{5,7},{6,4},{7,5},{8,10},{9,11},{10,... | collective-permute-start | bytes 522248 | tf_op jit(solution)/shard_map/ppermute | solution.py:26
  320.1 29.1 %collective-permute-start.20 = (bf16[2,576,768]{2,1,0:T(8,128)(2,1)}, bf16[2,576,768]{2,1,0:T(8,128)(2,1)}, u32[]{:S(2)}, u32[]{:S(2)}) collective-permute-start(bf16[2,576,768]{2,1,0:T(8,128)(2,1)} %dynamic-slice_bitcast_fusion.1), channel_id=1, source_target_pairs={{0,1},{1,0},{2,3},{3,2},{4,5},{5,4},{6,7},{7,6},{8,9},{9,8},{10,11... | collective-permute-start | bytes 5308424 | tf_op jit(solution)/shard_map/ppermute | solution.py:26
  321.3 31.2 %collective-permute-start.21 = (bf16[2,192,768]{2,1,0:T(8,128)(2,1)}, bf16[2,192,768]{2,1,0:T(8,128)(2,1)}, u32[]{:S(2)}, u32[]{:S(2)}) collective-permute-start(bf16[2,192,768]{2,1,0:T(8,128)(2,1)} %dynamic-slice_bitcast_fusion.4), channel_id=1, source_target_pairs={{0,1},{1,0},{2,3},{3,2},{4,5},{5,4},{6,7},{7,6},{8,9},{9,8},{10,11... | collective-permute-start | bytes 1769480 | tf_op jit(solution)/shard_map/ppermute | solution.py:26
  327.6 11.9 %copy-start.52 = (pred[2,512]{1,0:T(4,128)(4,1)S(1)}, pred[2,512]{1,0:T(4,128)(4,1)}, u32[]{:S(2)}) copy-start(pred[2,512]{1,0:T(4,128)(4,1)} %copy-done.51) | copy-start | bytes 3076
  328.4 1.9 collective-permute-start.25
  330.3 2.9 collective-permute-start.12
  333.2 3.3 collective-permute-start.13
  336.6 4.4 collective-permute-start.24
  341.0 13.6 %collective-permute-start.22 = (bf16[2,192,768]{2,1,0:T(8,128)(2,1)S(1)}, bf16[2,192,768]{2,1,0:T(8,128)(2,1)S(1)}, u32[]{:S(2)}, u32[]{:S(2)}) collective-permute-start(bf16[2,192,768]{2,1,0:T(8,128)(2,1)S(1)} %dynamic-slice_bitcast_fusion.3), channel_id=1, source_target_pairs={{0,1},{1,0},{2,3},{3,2},{4,5},{5,4},{6,7},{7,6},{8,9},{9,8},{10,11... | collective-permute-start | bytes 1769480 | tf_op jit(solution)/shard_map/ppermute | solution.py:26
  342.5 13.1 %collective-permute-start.23 = (bf16[2,192,768]{2,1,0:T(8,128)(2,1)}, bf16[2,192,768]{2,1,0:T(8,128)(2,1)S(1)}, u32[]{:S(2)}, u32[]{:S(2)}) collective-permute-start(bf16[2,192,768]{2,1,0:T(8,128)(2,1)} %dynamic-slice_bitcast_fusion.2), channel_id=1, source_target_pairs={{0,1},{1,0},{2,3},{3,2},{4,5},{5,4},{6,7},{7,6},{8,9},{9,8},{10,11... | collective-permute-start | bytes 1769480 | tf_op jit(solution)/shard_map/ppermute | solution.py:26
  (63 other events, 254.5 us)
